TPU v7x, 32 devices: a whole 2x2x4 slice. The times are simulated.
32 devices in a mesh: ctx: 4 (over y, x), ep: 8 (over z, core).
Axes of the slice: x: 2, y: 2, z: 4, core: 2. Of those that a mesh axis runs over, the one named last changes fastest.
Arguments:
- queries: bfloat16 [8, 512, 4096], P('ep', 'ctx'), may hold values from -150 to 150
- key_heads: bfloat16 [8, 512, 256], P('ep', 'ctx'), may hold values from -6 to 6
- value_head_array: bfloat16 [8, 512, 256], P('ep', 'ctx'), may hold values from -18 to 18
- trace_lengths: int32 [8, 6], P('ep'), may hold values from 1 to 128, 512 in all within a row
- expert_ids: int32 [8, 512, 8], P('ep', 'ctx'), may hold values from 0 to 127, all different within a row; in each aligned block of 128 rows (0 to 127, 128 to 255, ..., all dimensions but the last counted through in order) at most 10 rows name the same one
- gate_weights: float32 [8, 512, 8], P('ep', 'ctx'), may hold values from 0.1 to 1
- norm_gain: bfloat16 [4096], replicated, may hold values from 0.099609375 to 1.8984375
- w_gate: bfloat16 [4096, 12288], P('ctx', 'ep'), may hold values from -0.09375 to 0.09375
- w_up: bfloat16 [4096, 12288], P('ctx', 'ep'), may hold values from -0.09375 to 0.09375
- w_down: bfloat16 [12288, 4096], P('ep', 'ctx'), may hold values from -0.15625 to 0.15625
Outputs:
- layer_out: bfloat16 [8, 512, 4096], P('ep', 'ctx')
Inputs may be any that keep to these rules, and one draw needn't show every extreme that they name: `expert_ids`: the 8 ids of a row differ; among the 128 rows of one device no id is named more than 10 times.
All inputs are finite; a program needn't handle non-finite values.
Results may differ from a plain program's by a relative error of at most 0.0042.
Values may be sent and summed in bfloat16 or wider, within the bound.
A program may use at most 128 MiB of HBM per device.

v0:
```python
import math

import jax
import jax.numpy as jnp
from jax import lax
from jax.sharding import PartitionSpec as P

D = 4096
HEAD_SIZE = 128
QUERY_HEADS = 32
KEY_VALUE_HEADS = 2
EXP_WIN = 8
CAP = 10


def shifted(block, axis, distance):
    devices = range(lax.axis_size(axis))
    route = [(i - distance, i) for i in devices if i - distance in devices]
    return lax.ppermute(block, axis, route)


def trace_first(trace_lengths, positions):
    trace_ends = jnp.cumsum(trace_lengths)
    starts = trace_ends - trace_lengths
    return jnp.max(jnp.where(starts[None, :] <= positions[:, None], starts[None, :], 0), axis=1)


def fetch_weights(w_gate, w_up, w_down):
    gate_full, up_full = (
        lax.all_gather(w_gate, "ctx", axis=0, tiled=True),
        lax.all_gather(w_up, "ctx", axis=0, tiled=True),
    )
    down_full = lax.all_gather(w_down, "ctx", axis=1, tiled=True)
    return (gate_full, up_full, down_full)


def local(
    queries,
    key_heads,
    value_head_array,
    trace_lengths,
    expert_ids,
    gate_weights,
    norm_gain,
    w_gate,
    w_up,
    w_down,
):
    fetched = None
    rows_per_shard = queries.shape[1]
    head_groups = QUERY_HEADS // KEY_VALUE_HEADS
    ctx_place = lax.axis_index("ctx")
    ctx_count = lax.axis_size("ctx")
    reach_count = ctx_count // 4
    query_pos = ctx_place * rows_per_shard + jnp.arange(rows_per_shard, dtype=jnp.int32)
    first_pos = trace_first(trace_lengths[0], query_pos)
    query_division = queries[0].reshape(rows_per_shard, KEY_VALUE_HEADS, head_groups, HEAD_SIZE)
    score_scale = 1.0 / math.sqrt(HEAD_SIZE)

    def attend(running, kv_piece, offset):
        key_portion, value_portion = kv_piece
        width = key_portion.shape[1]
        size_value = min(512, width)
        old_max, old_total, old_sum = running
        key_division = key_portion[0, 0:size_value].reshape(size_value, KEY_VALUE_HEADS, HEAD_SIZE)
        value_division = value_portion[0, 0:size_value].reshape(
            size_value, KEY_VALUE_HEADS, HEAD_SIZE
        )
        scores = (
            jnp.einsum(
                "tkgd,skd->kgts", query_division, key_division, preferred_element_type=jnp.float32
            )
            * score_scale
        )
        key_pos = offset + 0 + jnp.arange(size_value, dtype=jnp.int32)
        visible = (key_pos[None, :] <= query_pos[:, None]) & (
            key_pos[None, :] >= first_pos[:, None]
        )
        scores = jnp.where(visible, scores, -1e30)
        new_max = jnp.maximum(old_max, jnp.max(scores, axis=-1))
        weights = jnp.where(visible, jnp.exp(scores - new_max[..., None]), 0.0)
        rescale = jnp.exp(old_max - new_max)
        new_total = old_total * rescale + jnp.sum(weights, axis=-1)
        new_sum = old_sum * rescale[..., None] + jnp.einsum(
            "kgts,skd->kgtd",
            weights.astype(jnp.bfloat16),
            value_division,
            preferred_element_type=jnp.float32,
        )
        running = (new_max, new_total, new_sum)
        return running

    empty_state = (
        jnp.full((KEY_VALUE_HEADS, head_groups, rows_per_shard), -1e30, jnp.float32),
        jnp.zeros((KEY_VALUE_HEADS, head_groups, rows_per_shard), jnp.float32),
        jnp.zeros((KEY_VALUE_HEADS, head_groups, rows_per_shard, HEAD_SIZE), jnp.float32),
    )
    own_pair = jnp.stack([key_heads, value_head_array])
    own_state = attend(empty_state, (key_heads, value_head_array), ctx_place * rows_per_shard)

    def earlier_step(i, state):
        moving, running = state
        moving = shifted(moving, "ctx", 1)
        running = attend(running, (moving[0], moving[1]), (ctx_place - i - 1) * rows_per_shard)
        return (moving, running)

    final_state = lax.fori_loop(0, reach_count, earlier_step, (own_pair, own_state))[1]
    context = (
        (final_state[2] / final_state[1][..., None])
        .transpose(2, 0, 1, 3)
        .reshape(rows_per_shard, QUERY_HEADS * HEAD_SIZE)
    )
    mean_square = jnp.mean(context * context, axis=-1, keepdims=True)
    normed = (context * lax.rsqrt(mean_square + 1e-06) * norm_gain.astype(jnp.float32)).astype(
        jnp.bfloat16
    )
    fetched = fetch_weights(w_gate, w_up, w_down)
    gate_full, up_full, down_full = fetched
    chosen_ids = expert_ids[0]
    weight_rows = gate_weights[0]
    slot_range = jnp.arange(CAP, dtype=jnp.int32)
    placing_list = []
    mixing_list = []
    for e in range(EXP_WIN):
        chosen = chosen_ids == e
        routed = jnp.any(chosen, axis=-1)
        gate_value = jnp.sum(jnp.where(chosen, weight_rows, 0.0), axis=-1)
        slot_index = jnp.cumsum(routed.astype(jnp.int32)) - 1
        taken = (slot_index[None, :] == slot_range[:, None]) & routed[None, :]
        placing_list.append(taken.astype(jnp.bfloat16))
        mixing_list.append(jnp.where(taken.T, gate_value[:, None], 0.0))
    placing = jnp.concatenate(placing_list, axis=0)
    mixing = jnp.concatenate(mixing_list, axis=1)
    stacked = (
        jnp.dot(placing, normed, preferred_element_type=jnp.float32)
        .astype(jnp.bfloat16)
        .reshape(EXP_WIN, CAP, D)
    )
    ep_count = lax.axis_size("ep")
    slab_size = ep_count // EXP_WIN
    outgoing = jnp.repeat(stacked, slab_size, axis=0)
    arrived = lax.all_to_all(outgoing, "ep", split_axis=0, concat_axis=0, tiled=True)
    flat_rows = arrived.reshape(-1, D)
    gate_proj = jnp.dot(flat_rows, gate_full, preferred_element_type=jnp.float32)
    up_proj = jnp.dot(flat_rows, up_full, preferred_element_type=jnp.float32)
    hidden = (jax.nn.silu(gate_proj) * up_proj).astype(jnp.bfloat16)
    partial_value = jnp.dot(hidden, down_full, preferred_element_type=jnp.float32).astype(
        jnp.bfloat16
    )
    returned = lax.all_to_all(
        partial_value.reshape(arrived.shape), "ep", split_axis=0, concat_axis=0, tiled=True
    )
    expert_out = returned.astype(jnp.float32).reshape(EXP_WIN, slab_size, CAP, D).sum(axis=1)
    expert_mix = jnp.dot(
        mixing,
        expert_out.reshape(EXP_WIN * CAP, D),
        precision=lax.Precision.HIGHEST,
        preferred_element_type=jnp.float32,
    )
    return (context + expert_mix).astype(jnp.bfloat16)[None]


def solution(mesh):
    in_specs = (
        P("ep", "ctx", None),
        P("ep", "ctx", None),
        P("ep", "ctx", None),
        P("ep", None),
        P("ep", "ctx", None),
        P("ep", "ctx", None),
        P(),
        P("ctx", "ep"),
        P("ctx", "ep"),
        P("ep", "ctx"),
    )
    out_specs = P("ep", "ctx", None)
    return jax.shard_map(local, mesh=mesh, in_specs=in_specs, out_specs=out_specs, check_vma=False)
```

profile of v0, /device:TPU:0, one launch (start us, length us, event | category | flops | bytes accessed | tf_op | source)
XLA Modules:
  0.0 438.9 jit_solution(1140171293155805119)
XLA Ops:
  6.5 0.7 all-gather.4.cloned.1.call-update
  7.3 0.0 all-gather.6.cloned.1.call-start
  7.3 0.7 all-gather.6.cloned.1.call-update
  8.1 0.7 all-gather.8.cloned.1.call-update
  8.8 0.1 copy-done.2
  8.9 0.1 copy.71
  9.0 0.1 copy.49
  9.1 0.7 pad_maximum_fusion
  9.8 4.8 %collective-permute-start = (bf16[2,1,128,256]{2,3,1,0:T(8,128)(2,1)}, bf16[2,1,128,256]{2,3,1,0:T(8,128)(2,1)S(1)}, u32[]{:S(2)}, u32[]{:S(2)}) collective-permute-start(bf16[2,1,128,256]{2,3,1,0:T(8,128)(2,1)} %pad_maximum_fusion), channel_id=1, source_target_pairs={{0,8},{8,16},{16,24},{1,9},{9,17},{17,25},{2,10},{10,18},{18,26},{... | collective-permute-start | bytes 393224 | tf_op jit(solution)/shard_map/while/body/eval_jaxpr/ppermute | solution.py:19
  14.7 0.2 copy.74
  14.9 0.6 fusion.74
  15.6 0.1 copy.57
  15.7 0.2 reduce-window_clone.1
  15.9 0.2 reduce-window.68
  16.1 0.1 copy.56
  16.2 0.2 reduce-window.67
  16.4 0.1 copy.59
  16.5 0.2 reduce-window.70
  16.7 0.1 copy.58
  16.8 0.2 reduce-window.69
  17.0 0.1 copy.61
  17.1 0.2 reduce-window.72
  17.3 0.1 copy.60
  17.4 0.2 reduce-window.71
  17.5 0.1 copy.55
  17.7 0.2 reduce-window.66
  17.8 0.1 copy.54
  18.0 0.2 reduce-window.65
  18.2 0.1 select_reduce_fusion.8
  18.3 0.1 add_reduce_fusion.4
  18.4 0.1 add_reduce_fusion.5
  18.5 0.1 add_reduce_fusion.2
  18.6 0.1 add_reduce_fusion.3
  18.7 0.1 add_reduce_fusion
  18.8 0.1 add_reduce_fusion.1
  19.0 0.1 add_reduce_fusion.6
  19.1 0.1 add_reduce_fusion.7
  19.3 0.1 compare_and_fusion
  19.4 0.7 fusion.5
  20.1 0.8 concatenate.10
  20.9 0.6 fusion.6
  21.6 1.3 fusion.7
  22.9 0.7 fusion.12
  23.6 1.0 multiply_reduce_fusion
  24.5 1.8 convolution_convert_fusion.1
  26.3 1.3 reshape_broadcast_in_dim_reshape.3
  27.6 31.4 %all_to_all.10 = bf16[8,10,4096]{2,1,0:T(8,128)(2,1)} all-to-all(bf16[8,10,4096]{2,1,0:T(8,128)(2,1)S(1)} %reshape_broadcast_in_dim_reshape.3), channel_id=1, replica_groups=mesh['ctx'=4,'ep'=8] {'ep'}, dimensions={0} | all-to-all | bytes 1310720 | tf_op jit(solution)/shard_map/all_to_all | solution.py:142
  59.0 1.5 reshape.379
  60.5 74.0 %all-gather.4.cloned.1.call-done = bf16[4096,1536]{1,0:T(8,128)(2,1)} async-done(((bf16[1024,1536]{1,0:T(8,128)(2,1)}), bf16[4096,1536]{1,0:T(8,128)(2,1)}) %all-gather.4.cloned.1.call-update) | async-done | bytes 12582928 | tf_op jit(solution)/shard_map/all_gather | solution.py:30
  134.4 7.6 %fusion.83 = f32[80,1536]{1,0:T(8,128)} fusion(bf16[80,4096]{1,0:T(8,128)(2,1)S(1)} %reshape.379, bf16[4096,1536]{1,0:T(8,128)(2,1)} %all-gather.4.cloned.1.call-done), kind=kOutput, calls=%fused_computation.153 | convolution fusion | flops 1006632960 | bytes 13729792 | tf_op jit(solution)/shard_map/dot_general | solution.py:144
  142.1 116.8 %all-gather.6.cloned.1.call-done = bf16[4096,1536]{1,0:T(8,128)(2,1)} async-done(((bf16[1024,1536]{1,0:T(8,128)(2,1)}), bf16[4096,1536]{1,0:T(8,128)(2,1)}) %all-gather.6.cloned.1.call-update) | async-done | bytes 12582928 | tf_op jit(solution)/shard_map/all_gather | solution.py:31
  258.8 124.4 %all-gather.8.cloned.1.call-done = bf16[1536,4096]{1,0:T(8,128)(2,1)} async-done(((bf16[1536,1024]{1,0:T(8,128)(2,1)}), bf16[1536,4096]{1,0:T(8,128)(2,1)}) %all-gather.8.cloned.1.call-update) | async-done | bytes 12582928 | tf_op jit(solution)/shard_map/all_gather | solution.py:33
  383.2 12.8 %convolution_convert_fusion = bf16[80,4096]{1,0:T(8,128)(2,1)S(1)} fusion(bf16[1536,4096]{1,0:T(8,128)(2,1)} %all-gather.8.cloned.1.call-done, bf16[80,4096]{1,0:T(8,128)(2,1)S(1)} %reshape.379, bf16[4096,1536]{1,0:T(8,128)(2,1)} %all-gather.6.cloned.1.call-done, f32[80,1536]{1,0:T(8,128)} %fusion.83), kind=kOutput, calls=%fused_computation.3 | convolution fusion | flops 2014330880 | bytes 26968064 | tf_op jit(solution)/shard_map/dot_general | solution.py:147
  396.1 1.2 reshape.380
  397.3 4.6 %all-to-all-start.1 = ((bf16[8,10,4096]{2,1,0:T(8,128)(2,1)}), bf16[8,10,4096]{2,1,0:T(8,128)(2,1)S(1)}, u32[]{:S(2)}, u32[]{:S(2)}) async-start(bf16[8,10,4096]{2,1,0:T(8,128)(2,1)} %reshape.380), calls=%async_computation.1 | async-start | bytes 2097152 | tf_op jit(solution)/shard_map/all_to_all | solution.py:150
  402.1 0.2 fusion.38
  402.2 0.2 fusion.42
  402.4 0.8 fusion.46
  403.2 0.8 fusion.50
  404.0 1.1 concatenate.9
  405.1 1.9 copy.62
  407.0 21.5 %all-to-all-done.1 = bf16[8,10,4096]{2,1,0:T(8,128)(2,1)S(1)} async-done(((bf16[8,10,4096]{2,1,0:T(8,128)(2,1)}), bf16[8,10,4096]{2,1,0:T(8,128)(2,1)S(1)}, u32[]{:S(2)}, u32[]{:S(2)}) %all-to-all-start.1) | async-done | bytes 655392 | tf_op jit(solution)/shard_map/all_to_all | solution.py:150
  428.5 0.2 reshape.381
  428.8 3.6 fusion.1
  (74 shorter events, 0.3 us)
Async XLA Ops:
  6.5 127.9 %all-gather.4.cloned.1.call-start = ((), (), s32[]{:S(2)}) async-start(), calls=%async_computation.2 | async-start | bytes 15728640 | tf_op jit(solution)/shard_map/all_gather | solution.py:30
  7.3 251.6 %all-gather.6.cloned.1.call-start = ((), (), s32[]{:S(2)}) async-start(), calls=%async_computation.3 | async-start | bytes 15728640 | tf_op jit(solution)/shard_map/all_gather | solution.py:31
  8.0 0.8 copy-start.2
  8.0 1.0 copy-start.1
  8.0 6.6 %copy-start = (bf16[1,128,4096]{2,1,0:T(8,128)(2,1)S(1)}, bf16[1,128,4096]{2,1,0:T(8,128)(2,1)}, u32[]{:S(2)}) copy-start(bf16[1,128,4096]{2,1,0:T(8,128)(2,1)} %param.10) | copy-start | bytes 3145732
  8.0 375.2 %all-gather.8.cloned.1.call-start = ((), (), s32[]{:S(2)}) async-start(), calls=%async_computation.4 | async-start | bytes 15728640 | tf_op jit(solution)/shard_map/all_gather | solution.py:33
  8.8 6.1 %copy-start.22 = (s32[1,128,8]{1,2,0:T(8,128)S(1)}, s32[1,128,8]{1,2,0:T(8,128)}, u32[]{:S(2)}) copy-start(s32[1,128,8]{1,2,0:T(8,128)} %param.14) | copy-start | bytes 12292
  8.8 6.9 %copy-start.24 = (s32[1,6]{1,0:T(1,128)S(1)}, s32[1,6]{1,0:T(1,128)}, u32[]{:S(2)}) copy-start(s32[1,6]{1,0:T(1,128)} %param.13) | copy-start | bytes 76
  9.1 9.0 %copy-start.3 = (bf16[4096]{0:T(1024)(128)(2,1)S(1)}, bf16[4096]{0:T(1024)(128)(2,1)}, u32[]{:S(2)}) copy-start(bf16[4096]{0:T(1024)(128)(2,1)} %param.16) | copy-start | bytes 24580
  9.8 11.1 %collective-permute-start = (bf16[2,1,128,256]{2,3,1,0:T(8,128)(2,1)}, bf16[2,1,128,256]{2,3,1,0:T(8,128)(2,1)S(1)}, u32[]{:S(2)}, u32[]{:S(2)}) collective-permute-start(bf16[2,1,128,256]{2,3,1,0:T(8,128)(2,1)} %pad_maximum_fusion), channel_id=1, source_target_pairs={{0,8},{8,16},{16,24},{1,9},{9,17},{17,25},{2,10},{10,18},{18,26},{... | collective-permute-start | bytes 393224 | tf_op jit(solution)/shard_map/while/body/eval_jaxpr/ppermute | solution.py:19
  15.6 3.6 copy-start.8
  15.6 3.6 copy-start.10
  15.6 3.7 copy-start.4
  15.6 3.7 copy-start.6
  15.6 4.5 %copy-start.12 = (pred[128]{0:T(512)(128)(4,1)}, pred[128]{0:T(512)(128)(4,1)S(1)}, u32[]{:S(2)}) copy-start(pred[128]{0:T(512)(128)(4,1)S(1)} %get-tuple-element.76) | copy-start | bytes 388
  396.0 5.9 %copy-start.14 = (pred[1,128,8]{1,2,0:T(8,128)(4,1)S(1)}, pred[1,128,8]{1,2,0:T(8,128)(4,1)}, u32[]{:S(2)}) copy-start(pred[1,128,8]{1,2,0:T(8,128)(4,1)} %get-tuple-element.46) | copy-start | bytes 3076
  396.0 5.9 %copy-start.15 = (pred[1,128,8]{1,2,0:T(8,128)(4,1)S(1)}, pred[1,128,8]{1,2,0:T(8,128)(4,1)}, u32[]{:S(2)}) copy-start(pred[1,128,8]{1,2,0:T(8,128)(4,1)} %get-tuple-element.67) | copy-start | bytes 3076
  396.0 5.9 %copy-start.16 = (pred[1,128,8]{1,2,0:T(8,128)(4,1)S(1)}, pred[1,128,8]{1,2,0:T(8,128)(4,1)}, u32[]{:S(2)}) copy-start(pred[1,128,8]{1,2,0:T(8,128)(4,1)} %get-tuple-element.69) | copy-start | bytes 3076
  396.1 5.9 %copy-start.17 = (pred[1,128,8]{1,2,0:T(8,128)(4,1)S(1)}, pred[1,128,8]{1,2,0:T(8,128)(4,1)}, u32[]{:S(2)}) copy-start(pred[1,128,8]{1,2,0:T(8,128)(4,1)} %get-tuple-element.71) | copy-start | bytes 3076
  396.1 5.9 %copy-start.18 = (pred[1,128,8]{1,2,0:T(8,128)(4,1)S(1)}, pred[1,128,8]{1,2,0:T(8,128)(4,1)}, u32[]{:S(2)}) copy-start(pred[1,128,8]{1,2,0:T(8,128)(4,1)} %get-tuple-element.73) | copy-start | bytes 3076
  396.1 5.9 %copy-start.19 = (pred[1,128,8]{1,2,0:T(8,128)(4,1)S(1)}, pred[1,128,8]{1,2,0:T(8,128)(4,1)}, u32[]{:S(2)}) copy-start(pred[1,128,8]{1,2,0:T(8,128)(4,1)} %get-tuple-element.75) | copy-start | bytes 3076
  396.1 5.9 %copy-start.20 = (pred[1,128,8]{1,2,0:T(8,128)(4,1)S(1)}, pred[1,128,8]{1,2,0:T(8,128)(4,1)}, u32[]{:S(2)}) copy-start(pred[1,128,8]{1,2,0:T(8,128)(4,1)} %get-tuple-element.77) | copy-start | bytes 3076
  396.1 5.9 %copy-start.21 = (pred[1,128,8]{1,2,0:T(8,128)(4,1)S(1)}, pred[1,128,8]{1,2,0:T(8,128)(4,1)}, u32[]{:S(2)}) copy-start(pred[1,128,8]{1,2,0:T(8,128)(4,1)} %get-tuple-element.79) | copy-start | bytes 3076
  396.1 5.9 %copy-start.23 = (f32[1,128,8]{1,2,0:T(8,128)S(1)}, f32[1,128,8]{1,2,0:T(8,128)}, u32[]{:S(2)}) copy-start(f32[1,128,8]{1,2,0:T(8,128)} %param.15) | copy-start | bytes 12292
  396.1 5.9 %copy-start.13 = (pred[128]{0:T(512)(128)(4,1)S(1)}, pred[128]{0:T(512)(128)(4,1)}, u32[]{:S(2)}) copy-start(pred[128]{0:T(512)(128)(4,1)} %copy-done.12) | copy-start | bytes 388
  397.3 5.1 %copy-start.9 = (pred[128]{0:T(512)(128)(4,1)S(1)}, pred[128]{0:T(512)(128)(4,1)}, u32[]{:S(2)}) copy-start(pred[128]{0:T(512)(128)(4,1)} %copy-done.8) | copy-start | bytes 388
  397.3 5.1 %copy-start.11 = (pred[128]{0:T(512)(128)(4,1)S(1)}, pred[128]{0:T(512)(128)(4,1)}, u32[]{:S(2)}) copy-start(pred[128]{0:T(512)(128)(4,1)} %copy-done.10) | copy-start | bytes 388
  397.3 5.9 %copy-start.5 = (pred[128]{0:T(512)(128)(4,1)S(1)}, pred[128]{0:T(512)(128)(4,1)}, u32[]{:S(2)}) copy-start(pred[128]{0:T(512)(128)(4,1)} %copy-done.4) | copy-start | bytes 388
  397.3 5.9 %copy-start.7 = (pred[128]{0:T(512)(128)(4,1)S(1)}, pred[128]{0:T(512)(128)(4,1)}, u32[]{:S(2)}) copy-start(pred[128]{0:T(512)(128)(4,1)} %copy-done.6) | copy-start | bytes 388
  397.3 31.2 %all-to-all-start.1 = ((bf16[8,10,4096]{2,1,0:T(8,128)(2,1)}), bf16[8,10,4096]{2,1,0:T(8,128)(2,1)S(1)}, u32[]{:S(2)}, u32[]{:S(2)}) async-start(bf16[8,10,4096]{2,1,0:T(8,128)(2,1)} %reshape.380), calls=%async_computation.1 | async-start | bytes 2097152 | tf_op jit(solution)/shard_map/all_to_all | solution.py:150
Sparse Core Ops, SparseCore 0:
  9.2 125.2 all-gather.3
  136.3 122.5 all-gather.5
  260.7 122.5 all-gather.7
where the time goes:
time: 439 us
  waiting for transfers between devices  339 us (77%)
  blocking collectives  31.4 us (7%)
  matrix products  28.7 us (7%)
  between operations  13.7 us (3%)
  starting transfers between devices  9.53 us (2%)
  local copies, waits for them, and re-layouts  9.48 us (2%)
  other arithmetic  7.27 us (2%)
    all_gather x1, waiting for transfers between devices, fetch_weights(): down_full = lax.all_gather(w_down, 'ctx', axis=1, tiled=True)  124 us
    all_gather x1, waiting for transfers between devices, fetch_weights(): lax.all_gather(w_up, 'ctx', axis=0, tiled=True)  117 us
    all_gather x1, waiting for transfers between devices, fetch_weights(): lax.all_gather(w_gate, 'ctx', axis=0, tiled=True)  74 us
    all_to_all x1, blocking collectives, local(): lax.all_to_all(outgoing, 'ep', split_axis=0, concat_axis=0, tiled=True)  31.4 us
    all_to_all x1, waiting for transfers between devices, local(): lax.all_to_all(partial_value.reshape(arrived.shape), 'ep', split_axis=0,...  21.5 us
    dot_general x1, matrix products, local(): jnp.dot(hidden, down_full, preferred_element_type=jnp.float32)  12.8 us
  transfers between devices with their start and end apart: 5, of which 4 were waited for; matrix products, arithmetic and copies ran while one was open for 6% of the time, Pallas kernels for 0%

commit v1 on v0

--- a/solution.py
+++ b/solution.py
@@ -25,13 +25,31 @@
     return jnp.max(jnp.where(starts[None, :] <= positions[:, None], starts[None, :], 0), axis=1)
 
 
-def fetch_weights(w_gate, w_up, w_down):
-    gate_full, up_full = (
-        lax.all_gather(w_gate, "ctx", axis=0, tiled=True),
-        lax.all_gather(w_up, "ctx", axis=0, tiled=True),
+def experts(stacked, w_gate, w_up, w_down):
+    ep_count = lax.axis_size("ep")
+    ctx_count = lax.axis_size("ctx")
+    slab_size = ep_count // EXP_WIN
+    wide = w_gate.shape[0]
+    rows = ep_count * CAP
+    outgoing = jnp.repeat(stacked, slab_size, axis=0)
+    arrived = lax.all_to_all(outgoing, "ep", split_axis=0, concat_axis=0, tiled=True)
+    cut = arrived.reshape(rows, ctx_count, wide).transpose(1, 0, 2)
+    cut = lax.all_to_all(cut, "ctx", split_axis=0, concat_axis=0, tiled=True)
+    flat = cut.reshape(ctx_count * rows, wide)
+    gate_part = jnp.dot(flat, w_gate, preferred_element_type=jnp.float32).astype(jnp.bfloat16)
+    up_part = jnp.dot(flat, w_up, preferred_element_type=jnp.float32).astype(jnp.bfloat16)
+    both = jnp.stack([gate_part, up_part]).reshape(2, ctx_count, rows, -1)
+    both = lax.all_to_all(both, "ctx", split_axis=1, concat_axis=1, tiled=True)
+    proj = jnp.sum(both.astype(jnp.float32), axis=1)
+    hidden = (jax.nn.silu(proj[0]) * proj[1]).astype(jnp.bfloat16)
+    hidden = lax.all_gather(hidden, "ctx", axis=0, tiled=True)
+    out = jnp.dot(hidden, w_down, preferred_element_type=jnp.float32).astype(jnp.bfloat16)
+    out = lax.all_to_all(
+        out.reshape(ctx_count, rows, wide), "ctx", split_axis=0, concat_axis=0, tiled=True
     )
-    down_full = lax.all_gather(w_down, "ctx", axis=1, tiled=True)
-    return (gate_full, up_full, down_full)
+    out = out.transpose(1, 0, 2).reshape(ep_count, CAP, ctx_count * wide)
+    returned = lax.all_to_all(out, "ep", split_axis=0, concat_axis=0, tiled=True)
+    return returned.astype(jnp.float32).reshape(EXP_WIN, slab_size, CAP, D).sum(axis=1)
 
 
 def local(
@@ -46,7 +64,6 @@
     w_up,
     w_down,
 ):
-    fetched = None
     rows_per_shard = queries.shape[1]
     head_groups = QUERY_HEADS // KEY_VALUE_HEADS
     ctx_place = lax.axis_index("ctx")
@@ -114,8 +131,6 @@
     normed = (context * lax.rsqrt(mean_square + 1e-06) * norm_gain.astype(jnp.float32)).astype(
         jnp.bfloat16
     )
-    fetched = fetch_weights(w_gate, w_up, w_down)
-    gate_full, up_full, down_full = fetched
     chosen_ids = expert_ids[0]
     weight_rows = gate_weights[0]
     slot_range = jnp.arange(CAP, dtype=jnp.int32)
@@ -136,21 +151,7 @@
         .astype(jnp.bfloat16)
         .reshape(EXP_WIN, CAP, D)
     )
-    ep_count = lax.axis_size("ep")
-    slab_size = ep_count // EXP_WIN
-    outgoing = jnp.repeat(stacked, slab_size, axis=0)
-    arrived = lax.all_to_all(outgoing, "ep", split_axis=0, concat_axis=0, tiled=True)
-    flat_rows = arrived.reshape(-1, D)
-    gate_proj = jnp.dot(flat_rows, gate_full, preferred_element_type=jnp.float32)
-    up_proj = jnp.dot(flat_rows, up_full, preferred_element_type=jnp.float32)
-    hidden = (jax.nn.silu(gate_proj) * up_proj).astype(jnp.bfloat16)
-    partial_value = jnp.dot(hidden, down_full, preferred_element_type=jnp.float32).astype(
-        jnp.bfloat16
-    )
-    returned = lax.all_to_all(
-        partial_value.reshape(arrived.shape), "ep", split_axis=0, concat_axis=0, tiled=True
-    )
-    expert_out = returned.astype(jnp.float32).reshape(EXP_WIN, slab_size, CAP, D).sum(axis=1)
+    expert_out = experts(stacked, w_gate, w_up, w_down)
     expert_mix = jnp.dot(
         mixing,
         expert_out.reshape(EXP_WIN * CAP, D),

time: 439 us -> 188 us (0.43)
  waiting for transfers between devices: 339 us -> 20.4 us
  blocking collectives: 31.4 us -> 92 us
  local copies, waits for them, and re-layouts: 9.48 us -> 26.5 us
  other arithmetic: 7.27 us -> 22.6 us
  between operations: 13.7 us -> 0.64 us
  matrix products: 28.7 us -> 16.1 us
    all_gather x3 -> x0, waiting for transfers between devices: 315 us -> none  [the longest x1 124 us: fetch_weights(): down_full = lax.all_gather(w_down, 'ctx', axis=1, tiled=True)]
    all_to_all x1 -> x4, blocking collectives: 31.4 us -> 79.1 us  [the longest x1 31.6 us: experts(): lax.all_to_all(outgoing, 'ep', split_axis=0, concat_axis=0, tiled=True)]
    dot_general x2 -> x3, matrix products: 20.4 us -> 3.61 us  [the longest x1 1.24 us: experts(): jnp.dot(hidden, w_down, preferred_element_type=jnp.float32)]
    all_gather x0 -> x1, blocking collectives: none -> 12.9 us  [experts(): hidden = lax.all_gather(hidden, 'ctx', axis=0, tiled=True)]
    unnamed x52 -> x76, local copies, waits for them, and re-layouts: 0.53 us -> 6.13 us
  transfers between devices with their start and end apart: 5 -> 2, of which waited for: 4 -> 1; matrix products, arithmetic and copies ran while one was open for 6% -> 17% of each run, Pallas kernels for 0% -> 0%
where the time goes in v1:
time: 188 us; the launch traced here: 187 us
  blocking collectives  92 us (49%)
  local copies, waits for them, and re-layouts  26.5 us (14%)
  other arithmetic  22.6 us (12%)
  waiting for transfers between devices  20.4 us (11%)
  matrix products  16.1 us (9%)
  starting transfers between devices  9.07 us (5%)
    all_to_all x1, blocking collectives, experts(): lax.all_to_all(outgoing, 'ep', split_axis=0, concat_axis=0, tiled=True)  31.6 us
    all_to_all x1, blocking collectives, experts(): both = lax.all_to_all(both, 'ctx', split_axis=1, concat_axis=1, tiled=True)  24.9 us
    all_to_all x1, waiting for transfers between devices, experts(): lax.all_to_all(out, 'ep', split_axis=0, concat_axis=0, tiled=True)  20.4 us
    all_gather x1, blocking collectives, experts(): hidden = lax.all_gather(hidden, 'ctx', axis=0, tiled=True)  12.9 us
    all_to_all x1, blocking collectives, experts(): cut = lax.all_to_all(cut, 'ctx', split_axis=0, concat_axis=0, tiled=True)  12.2 us
    all_to_all x1, blocking collectives, experts(): lax.all_to_all(out.reshape(ctx_count, rows, wide), 'ctx', split_axis=0, c...  10.4 us
    unnamed x76, local copies, waits for them, and re-layouts  6.13 us
    dot_general x2, matrix products, attend(): jnp.einsum('tkgd,skd->kgts', query_division, key_division, preferred_elem...  5.26 us
  transfers between devices with their start and end apart: 2, of which 1 were waited for; matrix products, arithmetic and copies ran while one was open for 17% of the time, Pallas kernels for 0%

profile of v1, /device:TPU:0, one launch (start us, length us, event | category | flops | bytes accessed | tf_op | source)
XLA Modules:
  0.0 187.4 jit_solution(13145108336277385502)
XLA Ops:
  0.0 1.1 copy.99
  1.1 1.0 copy.73
  2.1 0.7 pad_maximum_fusion.1
  2.8 4.8 %collective-permute-start = (bf16[2,1,128,256]{2,3,1,0:T(8,128)(2,1)}, bf16[2,1,128,256]{2,3,1,0:T(8,128)(2,1)S(1)}, u32[]{:S(2)}, u32[]{:S(2)}) collective-permute-start(bf16[2,1,128,256]{2,3,1,0:T(8,128)(2,1)} %pad_maximum_fusion.1), channel_id=1, source_target_pairs={{0,8},{8,16},{16,24},{1,9},{9,17},{17,25},{2,10},{10,18},{18,26},{... | collective-permute-start | bytes 393224 | tf_op jit(solution)/shard_map/while/body/eval_jaxpr/ppermute | solution.py:19
  7.6 0.9 reshape_squeeze.9
  8.5 0.6 iota_add_fusion.1
  9.1 0.8 reduce-window_clone.1
  9.9 1.2 subtract_bitcast_fusion
  11.1 0.6 iota_add_fusion
  11.7 2.4 %copy.102 = bf16[16,8,32,128]{3,2,1,0:T(8,128)(2,1)} copy(bf16[16,8,32,128]{3,1,2,0:T(8,128)(2,1)} %bitcast.136) | data formatting | bytes 2097152
  14.1 1.2 fusion.68
  15.3 0.6 copy-done.20
  16.2 0.7 add_reduce_fusion.4
  16.9 0.7 convert_bitcast_fusion.5
  17.7 0.2 reduce-window.67
  17.8 0.6 add_reduce_fusion.5
  18.5 0.7 convert_bitcast_fusion.2
  19.4 0.7 add_reduce_fusion.2
  20.1 0.6 convert_bitcast_fusion.3
  20.8 0.2 reduce-window.69
  21.0 0.7 add_reduce_fusion.3
  22.0 0.7 add_reduce_fusion
  23.0 0.6 add_reduce_fusion.1
  23.6 0.6 convert_bitcast_fusion.6
  24.5 0.6 add_reduce_fusion.6
  25.2 0.6 convert_bitcast_fusion.7
  26.2 0.8 select_reduce_fusion.8
  27.0 0.8 compare_and_fusion
  27.8 0.7 fusion.54
  28.5 0.7 fusion.56
  29.2 0.7 fusion.58
  29.9 3.2 %fusion.4 = (f32[2,16,128]{2,1,0:T(8,128)S(1)}, f32[2,128,128,16]{2,1,3,0:T(8,128)}) fusion(pred[128,128]{0,1:T(8,128)(4,1)S(1)} %get-tuple-element.81, bf16[128,2,16,128]{3,2,1,0:T(8,128)(2,1)} %bitcast.130, bf16[128,2,128,1]{2,1,0,3:T(2,128)(2,1)S(1)} %bitcast.144), kind=kOutput, calls=%fused_computation.18 | convolution fusion | flops 135786496 | bytes 3244032 | tf_op jit(solution)/shard_map/tkgd,skd->kgts/dot_general | solution.py:87
  33.2 0.6 fusion.52
  33.8 0.8 concatenate.11
  34.6 2.0 %fusion.5 = (f32[2,16,128]{2,1,0:T(8,128)S(1)}, f32[2,128,128,16]{2,1,3,0:T(8,128)S(1)}) fusion(pred[128,128]{0,1:T(8,128)(4,1)S(1)} %get-tuple-element.80, bf16[128,2,128,1]{0,2,3,1:T(8,128)(2,1)S(1)} %bitcast.145, bf16[128,2,16,128]{3,2,1,0:T(8,128)(2,1)} %bitcast.131), kind=kOutput, calls=%fused_computation.19 | convolution fusion | flops 135786496 | bytes 3244032 | tf_op jit(solution)/shard_map/while/body/eval_jaxpr/tkgd,skd->kgts/dot_general | solution.py:87
  36.7 0.7 fusion.11
  37.4 1.3 fusion.6
  38.7 0.9 multiply_reduce_fusion
  39.6 1.3 copy-done.2
  41.0 1.8 convolution_convert_fusion
  42.8 2.3 %reshape_broadcast_in_dim_reshape.3 = bf16[8,10,4096]{2,1,0:T(8,128)(2,1)} reshape(bf16[80,4096]{1,0:T(8,128)(2,1)} %convolution_convert_fusion) | data formatting | bytes 1310720 | tf_op jit(solution)/shard_map/reshape;broadcast_in_dim;reshape | solution.py:34
  45.0 31.6 %all_to_all.25 = bf16[8,10,4096]{2,1,0:T(8,128)(2,1)} all-to-all(bf16[8,10,4096]{2,1,0:T(8,128)(2,1)} %reshape_broadcast_in_dim_reshape.3), channel_id=1, replica_groups=mesh['ctx'=4,'ep'=8] {'ep'}, dimensions={0} | all-to-all | bytes 1310720 | tf_op jit(solution)/shard_map/all_to_all | solution.py:35
  76.6 2.9 %reshape.390 = bf16[80,4,1024]{2,1,0:T(4,128)(2,1)} reshape(bf16[8,10,4096]{2,1,0:T(8,128)(2,1)} %all_to_all.25) | data formatting | bytes 1310720 | tf_op jit(solution)/shard_map/reshape | solution.py:36
  79.5 1.3 copy.86
  80.8 12.2 %all_to_all.26 = bf16[4,80,1024]{2,1,0:T(8,128)(2,1)S(1)} all-to-all(bf16[4,80,1024]{2,1,0:T(8,128)(2,1)S(1)} %copy.86), channel_id=1, replica_groups=mesh['ctx'=4,'ep'=8] {'ctx'}, dimensions={0} | all-to-all | bytes 1310720 | tf_op jit(solution)/shard_map/all_to_all | solution.py:37
  93.1 1.2 convolution_convert_fusion.2
  94.3 0.7 copy-done.35
  94.9 1.2 convolution_convert_fusion.1
  96.1 0.2 pad_maximum_fusion
  96.3 24.9 %all_to_all.27 = bf16[2,4,80,1536]{3,2,0,1:T(8,128)(2,1)S(1)} all-to-all(bf16[2,4,80,1536]{3,2,0,1:T(8,128)(2,1)S(1)} %pad_maximum_fusion), channel_id=1, replica_groups=mesh['ctx'=4,'ep'=8] {'ctx'}, dimensions={1} | all-to-all | bytes 3932160 | tf_op jit(solution)/shard_map/all_to_all | solution.py:42
  121.2 0.3 convert_reduce_fusion
  121.7 12.9 %all_gather.3 = bf16[320,1536]{1,0:T(8,128)(2,1)S(1)} all-gather(bf16[80,1536]{1,0:T(8,128)(2,1)S(1)} %fusion.30), channel_id=1, replica_groups=mesh['ctx'=4,'ep'=8] {'ctx'}, dimensions={0}, use_global_device_ids=true | all-gather | bytes 1228800 | tf_op jit(solution)/shard_map/all_gather | solution.py:45
  134.6 1.2 convolution_convert_fusion.3
  135.9 10.4 %all_to_all.28 = bf16[4,80,1024]{2,1,0:T(8,128)(2,1)S(1)} all-to-all(bf16[4,80,1024]{2,1,0:T(8,128)(2,1)S(1)} %bitcast.141), channel_id=1, replica_groups=mesh['ctx'=4,'ep'=8] {'ctx'}, dimensions={0} | all-to-all | bytes 1310720 | tf_op jit(solution)/shard_map/all_to_all | solution.py:47
  146.2 1.3 copy.89
  147.8 2.7 %reshape.393 = bf16[8,10,4096]{2,1,0:T(8,128)(2,1)} reshape(bf16[80,4,1024]{2,1,0:T(4,128)(2,1)} %copy.89) | data formatting | bytes 1310720 | tf_op jit(solution)/shard_map/reshape | solution.py:50
  150.5 4.2 %all-to-all-start.4 = ((bf16[8,10,4096]{2,1,0:T(8,128)(2,1)}), bf16[8,10,4096]{2,1,0:T(8,128)(2,1)}, u32[]{:S(2)}, u32[]{:S(2)}) async-start(bf16[8,10,4096]{2,1,0:T(8,128)(2,1)} %reshape.393), calls=%async_computation.4 | async-start | bytes 2097152 | tf_op jit(solution)/shard_map/all_to_all | solution.py:51
  155.3 0.8 fusion.41
  156.1 0.8 fusion.45
  156.9 1.1 concatenate.10
  158.0 2.9 %copy.90 = f32[128,4096]{1,0:T(8,128)} copy(f32[128,4096]{0,1:T(8,128)} %bitcast.133) | data formatting | bytes 4194304 | tf_op jit(solution)/shard_map/reshape | solution.py:128
  160.9 20.4 %all-to-all-done.4 = bf16[8,10,4096]{2,1,0:T(8,128)(2,1)} async-done(((bf16[8,10,4096]{2,1,0:T(8,128)(2,1)}), bf16[8,10,4096]{2,1,0:T(8,128)(2,1)}, u32[]{:S(2)}, u32[]{:S(2)}) %all-to-all-start.4) | async-done | bytes 655392 | tf_op jit(solution)/shard_map/all_to_all | solution.py:51
  181.3 2.3 %reshape.394 = bf16[80,4096]{1,0:T(8,128)(2,1)} reshape(bf16[8,10,4096]{2,1,0:T(8,128)(2,1)} %all-to-all-done.4) | data formatting | bytes 1310720 | tf_op jit(solution)/shard_map/reshape | solution.py:157
  183.6 3.8 %fusion.1 = bf16[1,128,4096]{2,1,0:T(8,128)(2,1)} fusion(f32[128,4096]{1,0:T(8,128)} %copy.90, f32[128,80]{1,0:T(8,128)S(1)} %concatenate.10, bf16[80,4096]{1,0:T(8,128)(2,1)} %reshape.394), kind=kOutput, calls=%fused_computation.2 | convolution fusion | flops 504365056 | bytes 3842048 | tf_op jit(solution)/shard_map/dot_general | solution.py:155
  (99 shorter events, 2.8 us)
Async XLA Ops:
  0.0 93.1 %copy-start = (bf16[1024,1536]{1,0:T(8,128)(2,1)S(1)}, bf16[1024,1536]{1,0:T(8,128)(2,1)}, u32[]{:S(2)}) copy-start(bf16[1024,1536]{1,0:T(8,128)(2,1)} %param.17) | copy-start | bytes 9437188
  0.0 14.1 %copy-start.33 = (s32[1,128,8]{1,2,0:T(8,128)S(1)}, s32[1,128,8]{1,2,0:T(8,128)}, u32[]{:S(2)}) copy-start(s32[1,128,8]{1,2,0:T(8,128)} %param.14) | copy-start | bytes 12292
  2.8 31.8 %collective-permute-start = (bf16[2,1,128,256]{2,3,1,0:T(8,128)(2,1)}, bf16[2,1,128,256]{2,3,1,0:T(8,128)(2,1)S(1)}, u32[]{:S(2)}, u32[]{:S(2)}) collective-permute-start(bf16[2,1,128,256]{2,3,1,0:T(8,128)(2,1)} %pad_maximum_fusion.1), channel_id=1, source_target_pairs={{0,8},{8,16},{16,24},{1,9},{9,17},{17,25},{2,10},{10,18},{18,26},{... | collective-permute-start | bytes 393224 | tf_op jit(solution)/shard_map/while/body/eval_jaxpr/ppermute | solution.py:19
  11.7 14.5 %copy-start.3 = (bf16[4096]{0:T(1024)(128)(2,1)S(1)}, bf16[4096]{0:T(1024)(128)(2,1)}, u32[]{:S(2)}) copy-start(bf16[4096]{0:T(1024)(128)(2,1)} %param.16) | copy-start | bytes 24580
  15.3 0.6 copy-start.20
  15.3 10.9 %copy-start.14 = (pred[128]{0:T(512)(128)(4,1)}, pred[128]{0:T(512)(128)(4,1)S(1)}, u32[]{:S(2)}) copy-start(pred[128]{0:T(512)(128)(4,1)S(1)} %get-tuple-element.45) | copy-start | bytes 388
  15.3 10.9 %copy-start.16 = (pred[128]{0:T(512)(128)(4,1)}, pred[128]{0:T(512)(128)(4,1)S(1)}, u32[]{:S(2)}) copy-start(pred[128]{0:T(512)(128)(4,1)S(1)} %get-tuple-element.78) | copy-start | bytes 388
  26.1 7.1 %copy-start.10 = (s32[128]{0:T(128)S(1)}, s32[128]{0:T(128)}, u32[]{:S(2)}) copy-start(s32[128]{0:T(128)} %add_reduce_fusion.6) | copy-start | bytes 1540
  26.2 7.6 %copy-start.12 = (s32[128]{0:T(128)}, s32[128]{0:T(128)S(1)}, u32[]{:S(2)}) copy-start(s32[128]{0:T(128)S(1)} %add_reduce_fusion.7) | copy-start | bytes 1540
  34.6 2.1 %copy-start.1 = (f32[2,128,128,16]{2,1,3,0:T(8,128)S(1)}, f32[2,128,128,16]{2,1,3,0:T(8,128)}, u32[]{:S(2)}) copy-start(f32[2,128,128,16]{2,1,3,0:T(8,128)} %get-tuple-element.85) | copy-start | bytes 6291460
  39.6 1.4 copy-start.2
  93.1 1.9 %copy-start.35 = (bf16[1024,1536]{1,0:T(8,128)(2,1)S(1)}, bf16[1024,1536]{1,0:T(8,128)(2,1)}, u32[]{:S(2)}) copy-start(bf16[1024,1536]{1,0:T(8,128)(2,1)} %param.18) | copy-start | bytes 9437188
  121.2 13.4 %copy-start.36 = (bf16[1536,1024]{1,0:T(8,128)(2,1)S(1)}, bf16[1536,1024]{1,0:T(8,128)(2,1)}, u32[]{:S(2)}) copy-start(bf16[1536,1024]{1,0:T(8,128)(2,1)} %param.19) | copy-start | bytes 9437188
  147.6 7.2 %copy-start.25 = (pred[1,128,8]{1,2,0:T(8,128)(4,1)S(1)}, pred[1,128,8]{1,2,0:T(8,128)(4,1)}, u32[]{:S(2)}) copy-start(pred[1,128,8]{1,2,0:T(8,128)(4,1)} %get-tuple-element.46) | copy-start | bytes 3076
  147.6 7.2 %copy-start.26 = (pred[1,128,8]{1,2,0:T(8,128)(4,1)S(1)}, pred[1,128,8]{1,2,0:T(8,128)(4,1)}, u32[]{:S(2)}) copy-start(pred[1,128,8]{1,2,0:T(8,128)(4,1)} %get-tuple-element.67) | copy-start | bytes 3076
  147.6 7.2 %copy-start.27 = (pred[1,128,8]{1,2,0:T(8,128)(4,1)S(1)}, pred[1,128,8]{1,2,0:T(8,128)(4,1)}, u32[]{:S(2)}) copy-start(pred[1,128,8]{1,2,0:T(8,128)(4,1)} %get-tuple-element.69) | copy-start | bytes 3076
  147.6 7.2 %copy-start.28 = (pred[1,128,8]{1,2,0:T(8,128)(4,1)S(1)}, pred[1,128,8]{1,2,0:T(8,128)(4,1)}, u32[]{:S(2)}) copy-start(pred[1,128,8]{1,2,0:T(8,128)(4,1)} %get-tuple-element.71) | copy-start | bytes 3076
  147.6 7.2 %copy-start.29 = (pred[1,128,8]{1,2,0:T(8,128)(4,1)S(1)}, pred[1,128,8]{1,2,0:T(8,128)(4,1)}, u32[]{:S(2)}) copy-start(pred[1,128,8]{1,2,0:T(8,128)(4,1)} %get-tuple-element.73) | copy-start | bytes 3076
  147.6 7.2 %copy-start.30 = (pred[1,128,8]{1,2,0:T(8,128)(4,1)S(1)}, pred[1,128,8]{1,2,0:T(8,128)(4,1)}, u32[]{:S(2)}) copy-start(pred[1,128,8]{1,2,0:T(8,128)(4,1)} %get-tuple-element.75) | copy-start | bytes 3076
  147.6 7.2 %copy-start.31 = (pred[1,128,8]{1,2,0:T(8,128)(4,1)S(1)}, pred[1,128,8]{1,2,0:T(8,128)(4,1)}, u32[]{:S(2)}) copy-start(pred[1,128,8]{1,2,0:T(8,128)(4,1)} %get-tuple-element.77) | copy-start | bytes 3076
  147.6 7.2 %copy-start.32 = (pred[1,128,8]{1,2,0:T(8,128)(4,1)S(1)}, pred[1,128,8]{1,2,0:T(8,128)(4,1)}, u32[]{:S(2)}) copy-start(pred[1,128,8]{1,2,0:T(8,128)(4,1)} %get-tuple-element.79) | copy-start | bytes 3076
  147.6 7.2 %copy-start.34 = (f32[1,128,8]{1,2,0:T(8,128)S(1)}, f32[1,128,8]{1,2,0:T(8,128)}, u32[]{:S(2)}) copy-start(f32[1,128,8]{1,2,0:T(8,128)} %param.15) | copy-start | bytes 12292
  147.6 7.2 %copy-start.11 = (s32[128]{0:T(128)S(1)}, s32[128]{0:T(128)}, u32[]{:S(2)}) copy-start(s32[128]{0:T(128)} %add_reduce_fusion.6) | copy-start | bytes 1540
  147.6 7.2 %copy-start.13 = (s32[128]{0:T(128)S(1)}, s32[128]{0:T(128)}, u32[]{:S(2)}) copy-start(s32[128]{0:T(128)} %copy-done.12) | copy-start | bytes 1540
  147.6 7.2 %copy-start.23 = (pred[128]{0:T(512)(128)(4,1)S(1)}, pred[128]{0:T(512)(128)(4,1)}, u32[]{:S(2)}) copy-start(pred[128]{0:T(512)(128)(4,1)} %get-tuple-element.74) | copy-start | bytes 388
  147.7 7.2 %copy-start.24 = (pred[128]{0:T(512)(128)(4,1)S(1)}, pred[128]{0:T(512)(128)(4,1)}, u32[]{:S(2)}) copy-start(pred[128]{0:T(512)(128)(4,1)} %get-tuple-element.76) | copy-start | bytes 388
  147.7 7.4 %copy-start.4 = (s32[128]{0:T(128)S(1)}, s32[128]{0:T(128)}, u32[]{:S(2)}) copy-start(s32[128]{0:T(128)} %add_reduce_fusion.4) | copy-start | bytes 1540
  147.7 7.4 %copy-start.6 = (s32[128]{0:T(128)S(1)}, s32[128]{0:T(128)}, u32[]{:S(2)}) copy-start(s32[128]{0:T(128)} %add_reduce_fusion.5) | copy-start | bytes 1540
  147.7 7.4 %copy-start.21 = (pred[128]{0:T(512)(128)(4,1)S(1)}, pred[128]{0:T(512)(128)(4,1)}, u32[]{:S(2)}) copy-start(pred[128]{0:T(512)(128)(4,1)} %copy-done.20) | copy-start | bytes 388
  147.7 7.4 %copy-start.22 = (pred[128]{0:T(512)(128)(4,1)S(1)}, pred[128]{0:T(512)(128)(4,1)}, u32[]{:S(2)}) copy-start(pred[128]{0:T(512)(128)(4,1)} %get-tuple-element.72) | copy-start | bytes 388
  147.7 7.6 %copy-start.5 = (s32[128]{0:T(128)S(1)}, s32[128]{0:T(128)}, u32[]{:S(2)}) copy-start(s32[128]{0:T(128)} %add_reduce_fusion.2) | copy-start | bytes 1540
  147.7 7.6 %copy-start.8 = (s32[128]{0:T(128)S(1)}, s32[128]{0:T(128)}, u32[]{:S(2)}) copy-start(s32[128]{0:T(128)} %add_reduce_fusion.3) | copy-start | bytes 1540
  147.7 7.6 %copy-start.18 = (pred[128]{0:T(512)(128)(4,1)S(1)}, pred[128]{0:T(512)(128)(4,1)}, u32[]{:S(2)}) copy-start(pred[128]{0:T(512)(128)(4,1)} %get-tuple-element.66) | copy-start | bytes 388
  147.7 7.6 %copy-start.19 = (pred[128]{0:T(512)(128)(4,1)S(1)}, pred[128]{0:T(512)(128)(4,1)}, u32[]{:S(2)}) copy-start(pred[128]{0:T(512)(128)(4,1)} %get-tuple-element.68) | copy-start | bytes 388
  147.7 8.3 %copy-start.7 = (s32[128]{0:T(128)S(1)}, s32[128]{0:T(128)}, u32[]{:S(2)}) copy-start(s32[128]{0:T(128)} %add_reduce_fusion) | copy-start | bytes 1540
  147.8 8.3 %copy-start.9 = (s32[128]{0:T(128)S(1)}, s32[128]{0:T(128)}, u32[]{:S(2)}) copy-start(s32[128]{0:T(128)} %add_reduce_fusion.1) | copy-start | bytes 1540
  147.8 8.3 %copy-start.15 = (pred[128]{0:T(512)(128)(4,1)S(1)}, pred[128]{0:T(512)(128)(4,1)}, u32[]{:S(2)}) copy-start(pred[128]{0:T(512)(128)(4,1)} %copy-done.14) | copy-start | bytes 388
  147.8 8.3 %copy-start.17 = (pred[128]{0:T(512)(128)(4,1)S(1)}, pred[128]{0:T(512)(128)(4,1)}, u32[]{:S(2)}) copy-start(pred[128]{0:T(512)(128)(4,1)} %copy-done.16) | copy-start | bytes 388
  150.5 30.8 %all-to-all-start.4 = ((bf16[8,10,4096]{2,1,0:T(8,128)(2,1)}), bf16[8,10,4096]{2,1,0:T(8,128)(2,1)}, u32[]{:S(2)}, u32[]{:S(2)}) async-start(bf16[8,10,4096]{2,1,0:T(8,128)(2,1)} %reshape.393), calls=%async_computation.4 | async-start | bytes 2097152 | tf_op jit(solution)/shard_map/all_to_all | solution.py:51

commit v2 on v1

--- a/solution.py
+++ b/solution.py
@@ -1,8 +1,12 @@
+import functools
 import math
 
 import jax
 import jax.numpy as jnp
+import numpy as np
 from jax import lax
+from jax.experimental import pallas as pl
+from jax.experimental.pallas import tpu as pltpu
 from jax.sharding import PartitionSpec as P
 
 D = 4096
@@ -52,7 +56,7 @@
     return returned.astype(jnp.float32).reshape(EXP_WIN, slab_size, CAP, D).sum(axis=1)
 
 
-def local(
+def local_plain(
     queries,
     key_heads,
     value_head_array,
@@ -161,6 +165,439 @@
     return (context + expert_mix).astype(jnp.bfloat16)[None]
 
 
+LANES = 128
+PIECES = 4
+MESH = pl.DeviceIdType.MESH
+
+
+def fused(
+    ctx_count,
+    ep_count,
+    ids_ref,
+    ids_t_ref,
+    gates_ref,
+    lengths_ref,
+    q_ref,
+    k_ref,
+    v_ref,
+    gain_ref,
+    row_meta_ref,
+    col_meta_ref,
+    lower_ref,
+    upper_ref,
+    perm_ref,
+    perm_t_ref,
+    w_gate_hbm,
+    w_up_hbm,
+    w_down_hbm,
+    out_ref,
+    kv_prev,
+    context,
+    normed,
+    tall,
+    sent_rows,
+    got_rows,
+    flat,
+    partial,
+    got_partial,
+    hidden,
+    got_hidden,
+    turned,
+    sent_out,
+    got_out,
+    expert_out,
+    w_gate,
+    w_up,
+    w_down,
+    w_sem,
+    kv_send,
+    kv_recv,
+    rows_send,
+    rows_recv,
+    part_send,
+    part_recv,
+    hid_send,
+    hid_recv,
+    out_send,
+    out_recv,
+):
+    f32, bf16 = jnp.float32, jnp.bfloat16
+    c = lax.axis_index("ctx")
+    e = lax.axis_index("ep")
+    devices = ctx_count * ep_count
+    tokens = q_ref.shape[0]
+    wide = w_gate.shape[0]
+    units = w_gate.shape[1]
+    chunks = wide // LANES
+    block = chunks * CAP
+    slots = ep_count * CAP
+    piece = units // PIECES
+    head_groups = QUERY_HEADS // KEY_VALUE_HEADS
+
+    weight_copies = [
+        pltpu.make_async_copy(hbm, vmem, w_sem.at[i])
+        for i, (hbm, vmem) in enumerate(
+            ((w_gate_hbm, w_gate), (w_up_hbm, w_up), (w_down_hbm, w_down))
+        )
+    ]
+    for copy in weight_copies:
+        copy.start()
+
+    def peer(i):
+        return lax.rem(c + i // ep_count, ctx_count), lax.rem(e + lax.rem(i, ep_count), ep_count)
+
+    barrier = pltpu.get_barrier_semaphore()
+
+    def greet(i, carry):
+        pl.semaphore_signal(barrier, inc=1, device_id=peer(i), device_id_type=MESH)
+        return carry
+
+    lax.fori_loop(1, devices, greet, 0)
+    pl.semaphore_wait(barrier, devices - 1)
+
+    kv_copies = [
+        pltpu.make_async_remote_copy(
+            src_ref=ref,
+            dst_ref=kv_prev.at[i],
+            send_sem=kv_send.at[i],
+            recv_sem=kv_recv.at[i],
+            device_id=(lax.rem(c + 1, ctx_count), e),
+            device_id_type=MESH,
+        )
+        for i, ref in enumerate((k_ref, v_ref))
+    ]
+    for copy in kv_copies:
+        copy.start()
+
+    named = jnp.zeros((ep_count * block, tokens), f32)
+    for j in range(ids_t_ref.shape[0]):
+        named += jnp.where(ids_t_ref[j : j + 1, :] == row_meta_ref[:, 0:1], 1.0, 0.0)
+    count = jnp.dot(named.astype(bf16), upper_ref[...], preferred_element_type=f32)
+    taken = jnp.where(count.astype(jnp.int32) == row_meta_ref[:, 2:3] + 1, named, 0.0)
+    for k in range(chunks):
+        tall[:, k * tokens : (k + 1) * tokens] = jnp.where(
+            row_meta_ref[:, 1:2] == k, taken, 0.0
+        ).astype(bf16)
+
+    query_pos = c * tokens + lax.broadcasted_iota(jnp.int32, (tokens, 2 * tokens), 0)
+    key_pos = (c - 1) * tokens + lax.broadcasted_iota(jnp.int32, (tokens, 2 * tokens), 1)
+    first_pos = jnp.zeros((tokens, 2 * tokens), jnp.int32)
+    start = jnp.int32(0)
+    for i in range(lengths_ref.shape[1]):
+        first_pos = jnp.where(query_pos >= start, start, first_pos)
+        start = start + lengths_ref[0, i]
+    visible = (key_pos <= query_pos) & (key_pos >= first_pos)
+    score_scale = 1.0 / math.sqrt(HEAD_SIZE)
+
+    for copy in kv_copies:
+        copy.wait()
+
+    for kv in range(KEY_VALUE_HEADS):
+        kv_cols = slice(kv * HEAD_SIZE, (kv + 1) * HEAD_SIZE)
+        keys = jnp.concatenate([kv_prev[0, :, kv_cols], k_ref[:, kv_cols]], axis=0)
+        values = jnp.concatenate([kv_prev[1, :, kv_cols], v_ref[:, kv_cols]], axis=0)
+
+        def attend(h, carry, kv=kv, keys=keys, values=values):
+            for one in range(4):
+                head = kv * head_groups + h * 4 + one
+                cols = pl.ds(pl.multiple_of(head * HEAD_SIZE, HEAD_SIZE), HEAD_SIZE)
+                scores = lax.dot_general(
+                    q_ref[:, cols], keys, (((1,), (1,)), ((), ())), preferred_element_type=f32
+                )
+                scores = jnp.where(visible, scores * score_scale, -1e30)
+                top = jnp.max(scores, axis=-1, keepdims=True)
+                weights = jnp.where(visible, jnp.exp(scores - top), 0.0)
+                total = jnp.sum(weights, axis=-1, keepdims=True)
+                summed = jnp.dot(weights.astype(bf16), values, preferred_element_type=f32)
+                context[:, cols] = summed / total
+            return carry
+
+        lax.fori_loop(0, head_groups // 4, attend, 0)
+
+    def add_square(h, running):
+        part = context[:, pl.ds(pl.multiple_of(h * HEAD_SIZE, HEAD_SIZE), HEAD_SIZE)]
+        return running + part * part
+
+    squares = lax.fori_loop(0, QUERY_HEADS, add_square, jnp.zeros((tokens, HEAD_SIZE), f32))
+    inverse = lax.rsqrt(jnp.sum(squares, axis=-1, keepdims=True) * (1.0 / D) + 1e-06)
+    for cc in range(ctx_count):
+        for k in range(chunks):
+            cols = slice(cc * wide + k * LANES, cc * wide + (k + 1) * LANES)
+            normed[k * tokens : (k + 1) * tokens, cc * LANES : (cc + 1) * LANES] = (
+                context[:, cols] * inverse * gain_ref[:, cols].astype(f32)
+            ).astype(bf16)
+
+    placed = jnp.dot(tall[...], normed[...], preferred_element_type=f32).astype(bf16)
+    for cc in range(ctx_count):
+        sent_rows[cc] = placed[:, cc * LANES : (cc + 1) * LANES]
+
+    me = c * ep_count + e
+
+    def rows_at(ref, cc, ee):
+        return ref.at[cc, pl.ds(pl.multiple_of(ee * block, 16), block), :]
+
+    def exchange(i, source, target, send_sem, recv_sem):
+        cc, ee = peer(i)
+        return pltpu.make_async_remote_copy(
+            src_ref=rows_at(source, cc, ee),
+            dst_ref=rows_at(target, c, e),
+            send_sem=send_sem.at[i],
+            recv_sem=recv_sem.at[me],
+            device_id=(cc, ee),
+            device_id_type=MESH,
+        )
+
+    def arrival(i, source, target, send_sem, recv_sem):
+        cc, ee = peer(i)
+        return pltpu.make_async_remote_copy(
+            src_ref=rows_at(source, cc, ee),
+            dst_ref=rows_at(target, cc, ee),
+            send_sem=send_sem.at[i],
+            recv_sem=recv_sem.at[cc * ep_count + ee],
+            device_id=(cc, ee),
+            device_id_type=MESH,
+        )
+
+    def all_exchange(source, target, send_sem, recv_sem):
+        def begin(i, carry):
+            exchange(i, source, target, send_sem, recv_sem).start()
+            return carry
+
+        lax.fori_loop(1, devices, begin, 0)
+        own = pl.ds(pl.multiple_of(e * block, 16), block)
+        target[c, own, :] = source[c, own, :]
+
+        def end(i, carry):
+            arrival(i, source, target, send_sem, recv_sem).wait_recv()
+            return carry
+
+        lax.fori_loop(1, devices, end, 0)
+
+    def all_sent(source, target, send_sem, recv_sem):
+        def end(i, carry):
+            exchange(i, source, target, send_sem, recv_sem).wait_send()
+            return carry
+
+        lax.fori_loop(1, devices, end, 0)
+
+    def unturned(ref):
+        cat = jnp.concatenate([ref[cc] for cc in range(ctx_count)], axis=1)
+        return jnp.dot(perm_ref[...], cat, preferred_element_type=f32).astype(bf16)
+
+    all_exchange(sent_rows, got_rows, rows_send, rows_recv)
+    ordered = unturned(got_rows)
+    for cc in range(ctx_count):
+        for k in range(chunks):
+            flat[cc * slots : (cc + 1) * slots, k * LANES : (k + 1) * LANES] = ordered[
+                k * slots : (k + 1) * slots, cc * LANES : (cc + 1) * LANES
+            ]
+
+    weight_copies[0].wait()
+    weight_copies[1].wait()
+    others = [lax.rem(c + d, ctx_count) for d in range(1, ctx_count)]
+
+    def part_copy(j, d, cc, slot):
+        return pltpu.make_async_remote_copy(
+            src_ref=partial.at[j, cc],
+            dst_ref=got_partial.at[j, slot],
+            send_sem=part_send.at[j, d],
+            recv_sem=part_recv.at[j, slot],
+            device_id=(cc, e),
+            device_id_type=MESH,
+        )
+
+    def hid_copy(j, d, cc, slot):
+        return pltpu.make_async_remote_copy(
+            src_ref=hidden.at[j],
+            dst_ref=got_hidden.at[j, slot],
+            send_sem=hid_send.at[j, d],
+            recv_sem=hid_recv.at[j, slot],
+            device_id=(cc, e),
+            device_id_type=MESH,
+        )
+
+    for j in range(PIECES):
+        cols = slice(j * piece, (j + 1) * piece)
+        gate = jnp.dot(flat[...], w_gate[:, cols], preferred_element_type=f32).astype(bf16)
+        up = jnp.dot(flat[...], w_up[:, cols], preferred_element_type=f32).astype(bf16)
+        for cc in range(ctx_count):
+            partial[j, cc, :, 0:piece] = gate[cc * slots : (cc + 1) * slots]
+            partial[j, cc, :, piece : 2 * piece] = up[cc * slots : (cc + 1) * slots]
+        for d, cc in enumerate(others):
+            part_copy(j, d, cc, c).start()
+
+    for j in range(PIECES):
+        proj = partial[j, c].astype(f32)
+        for d, cc in enumerate(others):
+            part_copy(j, d, cc, cc).wait_recv()
+            proj += got_partial[j, cc].astype(f32)
+        gate, up = proj[:, 0:piece], proj[:, piece : 2 * piece]
+        hidden[j] = (gate / (1.0 + jnp.exp(-gate)) * up).astype(bf16)
+        for d, cc in enumerate(others):
+            hid_copy(j, d, cc, c).start()
+        got_hidden[j, c] = hidden[j]
+
+    weight_copies[2].wait()
+    down = jnp.zeros((ctx_count * slots, wide), f32)
+    for j in range(PIECES):
+        for d, cc in enumerate(others):
+            hid_copy(j, d, cc, cc).wait_recv()
+        rows = jnp.concatenate([got_hidden[j, cc] for cc in range(ctx_count)], axis=0)
+        down += jnp.dot(
+            rows, w_down[j * piece : (j + 1) * piece, :], preferred_element_type=f32
+        )
+    down = down.astype(bf16)
+    for cc in range(ctx_count):
+        for k in range(chunks):
+            turned[k * slots : (k + 1) * slots, cc * LANES : (cc + 1) * LANES] = down[
+                cc * slots : (cc + 1) * slots, k * LANES : (k + 1) * LANES
+            ]
+    back = jnp.dot(perm_t_ref[...], turned[...], preferred_element_type=f32).astype(bf16)
+    for cc in range(ctx_count):
+        sent_out[cc] = back[:, cc * LANES : (cc + 1) * LANES]
+    all_exchange(sent_out, got_out, out_send, out_recv)
+    ordered = unturned(got_out)
+    for cc in range(ctx_count):
+        for k in range(chunks):
+            cols = slice(cc * wide + k * LANES, cc * wide + (k + 1) * LANES)
+            expert_out[:, cols] = ordered[k * slots : (k + 1) * slots, cc * LANES : (cc + 1) * LANES]
+
+    hits = jnp.zeros((tokens, slots), f32)
+    mix = jnp.zeros((tokens, slots), f32)
+    for j in range(ids_ref.shape[1]):
+        hit = ids_ref[:, j : j + 1] == col_meta_ref[0:1, :]
+        hits += jnp.where(hit, 1.0, 0.0)
+        mix += jnp.where(hit, gates_ref[:, j : j + 1], 0.0)
+    count = jnp.dot(lower_ref[...], hits.astype(bf16), preferred_element_type=f32)
+    mix = jnp.where(count.astype(jnp.int32) == col_meta_ref[1:2, :] + 1, mix, 0.0)
+    high = mix.astype(bf16)
+    low = (mix - high.astype(f32)).astype(bf16)
+    both = jnp.concatenate([high, low], axis=0)
+    for cc in range(ctx_count):
+        cols = slice(cc * wide, (cc + 1) * wide)
+        mixed = jnp.dot(both, expert_out[:, cols], preferred_element_type=f32)
+        out_ref[:, cols] = (context[:, cols] + mixed[0:tokens] + mixed[tokens:]).astype(bf16)
+
+    for copy_set in (
+        (sent_rows, got_rows, rows_send, rows_recv),
+        (sent_out, got_out, out_send, out_recv),
+    ):
+        all_sent(*copy_set)
+    for j in range(PIECES):
+        for d, cc in enumerate(others):
+            part_copy(j, d, cc, c).wait_send()
+            hid_copy(j, d, cc, c).wait_send()
+
+
+def local_fused(
+    queries,
+    key_heads,
+    value_head_array,
+    trace_lengths,
+    expert_ids,
+    gate_weights,
+    norm_gain,
+    w_gate,
+    w_up,
+    w_down,
+):
+    bf16 = jnp.bfloat16
+    ctx_count, ep_count = lax.axis_size("ctx"), lax.axis_size("ep")
+    tokens = queries.shape[1]
+    wide, units = w_gate.shape
+    chunks = wide // LANES
+    slots = ep_count * CAP
+    tall_rows = chunks * slots
+    n = np.arange(tall_rows)
+    row_e, row_k, row_s = n // (chunks * CAP), n // CAP % chunks, n % CAP
+    row_meta = np.stack([row_e, row_k, row_s], axis=1).astype(np.int32)
+    m = np.arange(slots)
+    col_meta = np.stack([m // CAP, m % CAP], axis=0).astype(np.int32)
+    lower = np.tril(np.ones((tokens, tokens), np.float32))
+    perm = np.zeros((tall_rows, tall_rows), np.float32)
+    perm[row_k * slots + row_e * CAP + row_s, n] = 1.0
+    vmem = pl.BlockSpec(memory_space=pltpu.VMEM)
+    anywhere = pl.BlockSpec(memory_space=pl.ANY)
+    dma = pltpu.SemaphoreType.DMA
+    devices = ctx_count * ep_count
+    piece = units // PIECES
+    across = ctx_count * LANES
+    out = pl.pallas_call(
+        functools.partial(fused, ctx_count, ep_count),
+        out_shape=jax.ShapeDtypeStruct((tokens, D), bf16),
+        in_specs=[vmem] * 3
+        + [pl.BlockSpec(memory_space=pltpu.SMEM)]
+        + [vmem] * 10
+        + [anywhere] * 3,
+        out_specs=vmem,
+        scratch_shapes=[
+            pltpu.VMEM((2, tokens, KEY_VALUE_HEADS * HEAD_SIZE), bf16),
+            pltpu.VMEM((tokens, D), jnp.float32),
+            pltpu.VMEM((chunks * tokens, across), bf16),
+            pltpu.VMEM((tall_rows, chunks * tokens), bf16),
+            pltpu.VMEM((ctx_count, tall_rows, LANES), bf16),
+            pltpu.VMEM((ctx_count, tall_rows, LANES), bf16),
+            pltpu.VMEM((ctx_count * slots, wide), bf16),
+            pltpu.VMEM((PIECES, ctx_count, slots, 2 * piece), bf16),
+            pltpu.VMEM((PIECES, ctx_count, slots, 2 * piece), bf16),
+            pltpu.VMEM((PIECES, slots, piece), bf16),
+            pltpu.VMEM((PIECES, ctx_count, slots, piece), bf16),
+            pltpu.VMEM((tall_rows, across), bf16),
+            pltpu.VMEM((ctx_count, tall_rows, LANES), bf16),
+            pltpu.VMEM((ctx_count, tall_rows, LANES), bf16),
+            pltpu.VMEM((slots, D), bf16),
+            pltpu.VMEM((wide, units), bf16),
+            pltpu.VMEM((wide, units), bf16),
+            pltpu.VMEM((units, wide), bf16),
+            dma((3,)),
+            dma((2,)),
+            dma((2,)),
+            dma((devices,)),
+            dma((devices,)),
+            dma((PIECES, ctx_count)),
+            dma((PIECES, ctx_count)),
+            dma((PIECES, ctx_count)),
+            dma((PIECES, ctx_count)),
+            dma((devices,)),
+            dma((devices,)),
+        ],
+        compiler_params=pltpu.CompilerParams(
+            collective_id=0, has_side_effects=True, vmem_limit_bytes=56 * 1024 * 1024
+        ),
+        cost_estimate=pl.CostEstimate(
+            flops=4_000_000_000, bytes_accessed=14_000_000, transcendentals=1_000_000
+        ),
+    )(
+        expert_ids[0],
+        expert_ids[0].T,
+        gate_weights[0],
+        trace_lengths,
+        queries[0],
+        key_heads[0],
+        value_head_array[0],
+        norm_gain[None],
+        row_meta,
+        col_meta,
+        lower.astype(bf16),
+        lower.T.astype(bf16),
+        perm.astype(bf16),
+        perm.T.astype(bf16),
+        w_gate,
+        w_up,
+        w_down,
+    )
+    return out[None]
+
+
+def local(*args):
+    ctx_count, ep_count = lax.axis_size("ctx"), lax.axis_size("ep")
+    wide, units = args[7].shape
+    aligned = (wide // LANES * CAP) % 16 == 0 and units % (PIECES * LANES) == 0
+    if ep_count == EXP_WIN and ctx_count == 4 and aligned:
+        return local_fused(*args)
+    return local_plain(*args)
+
+
 def solution(mesh):
     in_specs = (
         P("ep", "ctx", None),

time: 188 us -> 100 us (0.53)
  Pallas kernels: 0 us -> 93.5 us
  blocking collectives: 92 us -> 0 us
  other arithmetic: 22.6 us -> 0 us
  waiting for transfers between devices: 20.4 us -> 0 us
  local copies, waits for them, and re-layouts: 26.5 us -> 6.42 us
  matrix products: 16.1 us -> 0 us
  starting transfers between devices: 9.07 us -> 0 us
    pallas_call x0 -> x1, Pallas kernels: none -> 93.5 us  [local_fused(): pl.pallas_call(functools.partial(fused, ctx_count, ep_count), out_shape=j...]
    all_to_all x4 -> x0, blocking collectives: 79.1 us -> none  [the longest x1 31.6 us: experts(): lax.all_to_all(outgoing, 'ep', split_axis=0, concat_axis=0, tiled=True)]
    all_to_all x1 -> x0, waiting for transfers between devices: 20.4 us -> none  [experts(): lax.all_to_all(out, 'ep', split_axis=0, concat_axis=0, tiled=True)]
    dot_general x9 -> x0, matrix products: 16.1 us -> none  [the longest x2 5.26 us: attend(): jnp.einsum('tkgd,skd->kgts', query_division, key_division, preferred_elem...]
    all_gather x1 -> x0, blocking collectives: 12.9 us -> none  [experts(): hidden = lax.all_gather(hidden, 'ctx', axis=0, tiled=True)]
    reshape x4 -> x0, local copies, waits for them, and re-layouts: 10.7 us -> none  [the longest x1 2.88 us: local(): context = (final_state[2] / final_state[1][..., None]).transpose(2, 0, 1,...]
    ppermute x1 -> x0, starting transfers between devices: 4.84 us -> none  [shifted(): return lax.ppermute(block, axis, route)]
    sub x8 -> x0, other arithmetic: 4.79 us -> none  [local(): slot_index = jnp.cumsum(routed.astype(jnp.int32)) - 1]
  transfers between devices with their start and end apart: 2 -> 0, of which waited for: 1 -> 0; matrix products, arithmetic and copies ran while one was open for 17% -> 0% of each run, Pallas kernels for 0% -> 0%
where the time goes in v2:
time: 100 us; the launch traced here: 99.9 us
  Pallas kernels  93.5 us (94%)
  local copies, waits for them, and re-layouts  6.42 us (6%)
    pallas_call x1, Pallas kernels, local_fused(): pl.pallas_call(functools.partial(fused, ctx_count, ep_count), out_shape=j...  93.5 us
    unnamed x2, local copies, waits for them, and re-layouts  3.69 us

profile of v2, /device:TPU:0, one launch (start us, length us, event | category | flops | bytes accessed | tf_op | source)
XLA Modules:
  0.0 99.9 jit_solution(10665322685321519403)
XLA Ops:
  0.0 1.3 %broadcast_in_dim.6.gain_ref = bf16[1,4096]{1,0:T(2,128)(2,1)} reshape(bf16[4096]{0:T(1024)(128)(2,1)} %param.22) | data formatting | bytes 16384 | tf_op jit(solution)/shard_map/broadcast_in_dim | solution.py:578
  1.3 1.4 %copy.17 = f32[1,128,8]{2,1,0:T(8,128)} copy(f32[1,128,8]{1,2,0:T(8,128)} %param.21) | data formatting | bytes 8192 | tf_op args[5]
  2.7 1.4 %copy.18.ids_ref = s32[128,8]{1,0:T(8,128)} copy(s32[128,8]{0,1:T(8,128)} %bitcast.10) | data formatting | bytes 8192 | tf_op jit(solution)/shard_map/squeeze | solution.py:571
  4.1 93.5 %shard_map.154 = bf16[128,4096]{1,0:T(8,128)(2,1)} custom-call(s32[128,8]{1,0:T(8,128)} %copy.18.ids_ref, s32[8,128]{1,0:T(8,128)} %bitcast.11, f32[128,8]{1,0:T(8,128)} %bitcast.9, s32[1,6]{1,0:T(1,128)} %lengths_ref.1, bf16[128,4096]{1,0:T(8,128)(2,1)} %bitcast.12, bf16[128,256]{1,0:T(8,128)(2,1)} %bitcast.13, bf16[128,256]{1,0:T(8,128)(2,1)} %bitcast.14, ...), custom_call_target="tpu_custom_call" | custom-call | flops 4000000000 | bytes 14000000 | tf_op jit(solution)/shard_map/pallas_call | solution.py:525
  97.6 2.3 %copy.20 = bf16[1,128,4096]{2,1,0:T(8,128)(2,1)} copy(bf16[1,128,4096]{2,1,0:T(8,128)(2,1)} %bitcast.8) | data formatting | bytes 2097152

commit v3 on v2

--- a/solution.py
+++ b/solution.py
@@ -166,7 +166,8 @@
 
 
 LANES = 128
-PIECES = 4
+PIECES = 2
+SLOT_GROUPS = (6, 4)
 MESH = pl.DeviceIdType.MESH
 
 
@@ -174,7 +175,6 @@
     ctx_count,
     ep_count,
     ids_ref,
-    ids_t_ref,
     gates_ref,
     lengths_ref,
     q_ref,
@@ -182,11 +182,12 @@
     v_ref,
     gain_ref,
     row_meta_ref,
-    col_meta_ref,
-    lower_ref,
+    slot_meta_ref,
     upper_ref,
-    perm_ref,
-    perm_t_ref,
+    perm_a_ref,
+    perm_b_ref,
+    perm_t_a_ref,
+    perm_t_b_ref,
     w_gate_hbm,
     w_up_hbm,
     w_down_hbm,
@@ -206,6 +207,7 @@
     sent_out,
     got_out,
     expert_out,
+    mix,
     w_gate,
     w_up,
     w_down,
@@ -229,10 +231,16 @@
     wide = w_gate.shape[0]
     units = w_gate.shape[1]
     chunks = wide // LANES
-    block = chunks * CAP
     slots = ep_count * CAP
     piece = units // PIECES
     head_groups = QUERY_HEADS // KEY_VALUE_HEADS
+    groups = range(len(SLOT_GROUPS))
+    perms = (perm_a_ref, perm_b_ref)
+    perms_t = (perm_t_a_ref, perm_t_b_ref)
+    blocks = [chunks * size for size in SLOT_GROUPS]
+    bases = [ep_count * chunks * sum(SLOT_GROUPS[:g]) for g in groups]
+    slot_counts = [ep_count * size for size in SLOT_GROUPS]
+    slot_bases = [ep_count * sum(SLOT_GROUPS[:g]) for g in groups]
 
     weight_copies = [
         pltpu.make_async_copy(hbm, vmem, w_sem.at[i])
@@ -253,6 +261,16 @@
         return carry
 
     lax.fori_loop(1, devices, greet, 0)
+    named = jnp.zeros((chunks * slots, tokens), f32)
+    for j in range(ids_ref.shape[0]):
+        named += jnp.where(ids_ref[j : j + 1, :] == row_meta_ref[:, 0:1], 1.0, 0.0)
+    count = jnp.dot(named.astype(bf16), upper_ref[...], preferred_element_type=f32)
+    taken = jnp.where(count.astype(jnp.int32) == row_meta_ref[:, 2:3] + 1, named, 0.0)
+    for k in range(chunks):
+        tall[:, k * tokens : (k + 1) * tokens] = jnp.where(
+            row_meta_ref[:, 1:2] == k, taken, 0.0
+        ).astype(bf16)
+
     pl.semaphore_wait(barrier, devices - 1)
 
     kv_copies = [
@@ -269,15 +287,17 @@
     for copy in kv_copies:
         copy.start()
 
-    named = jnp.zeros((ep_count * block, tokens), f32)
-    for j in range(ids_t_ref.shape[0]):
-        named += jnp.where(ids_t_ref[j : j + 1, :] == row_meta_ref[:, 0:1], 1.0, 0.0)
-    count = jnp.dot(named.astype(bf16), upper_ref[...], preferred_element_type=f32)
-    taken = jnp.where(count.astype(jnp.int32) == row_meta_ref[:, 2:3] + 1, named, 0.0)
-    for k in range(chunks):
-        tall[:, k * tokens : (k + 1) * tokens] = jnp.where(
-            row_meta_ref[:, 1:2] == k, taken, 0.0
-        ).astype(bf16)
+    hits = jnp.zeros((slots, tokens), f32)
+    gate_at = jnp.zeros((slots, tokens), f32)
+    for j in range(ids_ref.shape[0]):
+        hit = ids_ref[j : j + 1, :] == slot_meta_ref[:, 0:1]
+        hits += jnp.where(hit, 1.0, 0.0)
+        gate_at += jnp.where(hit, gates_ref[j : j + 1, :], 0.0)
+    count = jnp.dot(hits.astype(bf16), upper_ref[...], preferred_element_type=f32)
+    gate_at = jnp.where(count.astype(jnp.int32) == slot_meta_ref[:, 1:2] + 1, gate_at, 0.0)
+    high = gate_at.astype(bf16)
+    mix[:, 0:tokens] = high
+    mix[:, tokens : 2 * tokens] = (gate_at - high.astype(f32)).astype(bf16)
 
     query_pos = c * tokens + lax.broadcasted_iota(jnp.int32, (tokens, 2 * tokens), 0)
     key_pos = (c - 1) * tokens + lax.broadcasted_iota(jnp.int32, (tokens, 2 * tokens), 1)
@@ -327,166 +347,202 @@
                 context[:, cols] * inverse * gain_ref[:, cols].astype(f32)
             ).astype(bf16)
 
-    placed = jnp.dot(tall[...], normed[...], preferred_element_type=f32).astype(bf16)
-    for cc in range(ctx_count):
-        sent_rows[cc] = placed[:, cc * LANES : (cc + 1) * LANES]
-
     me = c * ep_count + e
 
-    def rows_at(ref, cc, ee):
-        return ref.at[cc, pl.ds(pl.multiple_of(ee * block, 16), block), :]
-
-    def exchange(i, source, target, send_sem, recv_sem):
+    def rows_at(ref, g, cc, ee):
+        return ref.at[cc, pl.ds(pl.multiple_of(bases[g] + ee * blocks[g], 16), blocks[g]), :]
+
+    def exchange(g, i, source, target, send_sem, recv_sem):
         cc, ee = peer(i)
         return pltpu.make_async_remote_copy(
-            src_ref=rows_at(source, cc, ee),
-            dst_ref=rows_at(target, c, e),
-            send_sem=send_sem.at[i],
-            recv_sem=recv_sem.at[me],
+            src_ref=rows_at(source, g, cc, ee),
+            dst_ref=rows_at(target, g, c, e),
+            send_sem=send_sem.at[g, i],
+            recv_sem=recv_sem.at[g, me],
             device_id=(cc, ee),
             device_id_type=MESH,
         )
 
-    def arrival(i, source, target, send_sem, recv_sem):
+    def arrival(g, i, source, target, send_sem, recv_sem):
         cc, ee = peer(i)
         return pltpu.make_async_remote_copy(
-            src_ref=rows_at(source, cc, ee),
-            dst_ref=rows_at(target, cc, ee),
-            send_sem=send_sem.at[i],
-            recv_sem=recv_sem.at[cc * ep_count + ee],
+            src_ref=rows_at(source, g, cc, ee),
+            dst_ref=rows_at(target, g, cc, ee),
+            send_sem=send_sem.at[g, i],
+            recv_sem=recv_sem.at[g, cc * ep_count + ee],
             device_id=(cc, ee),
             device_id_type=MESH,
         )
 
-    def all_exchange(source, target, send_sem, recv_sem):
+    def send_all(g, source, target, send_sem, recv_sem):
         def begin(i, carry):
-            exchange(i, source, target, send_sem, recv_sem).start()
+            exchange(g, i, source, target, send_sem, recv_sem).start()
             return carry
 
         lax.fori_loop(1, devices, begin, 0)
-        own = pl.ds(pl.multiple_of(e * block, 16), block)
+        own = pl.ds(pl.multiple_of(bases[g] + e * blocks[g], 16), blocks[g])
         target[c, own, :] = source[c, own, :]
 
+    def receive_all(g, source, target, send_sem, recv_sem):
         def end(i, carry):
-            arrival(i, source, target, send_sem, recv_sem).wait_recv()
+            arrival(g, i, source, target, send_sem, recv_sem).wait_recv()
             return carry
 
         lax.fori_loop(1, devices, end, 0)
 
-    def all_sent(source, target, send_sem, recv_sem):
+    def all_sent(g, source, target, send_sem, recv_sem):
         def end(i, carry):
-            exchange(i, source, target, send_sem, recv_sem).wait_send()
+            exchange(g, i, source, target, send_sem, recv_sem).wait_send()
             return carry
 
         lax.fori_loop(1, devices, end, 0)
 
-    def unturned(ref):
-        cat = jnp.concatenate([ref[cc] for cc in range(ctx_count)], axis=1)
-        return jnp.dot(perm_ref[...], cat, preferred_element_type=f32).astype(bf16)
-
-    all_exchange(sent_rows, got_rows, rows_send, rows_recv)
-    ordered = unturned(got_rows)
-    for cc in range(ctx_count):
-        for k in range(chunks):
-            flat[cc * slots : (cc + 1) * slots, k * LANES : (k + 1) * LANES] = ordered[
-                k * slots : (k + 1) * slots, cc * LANES : (cc + 1) * LANES
-            ]
-
-    weight_copies[0].wait()
-    weight_copies[1].wait()
+    def unturned(g, ref):
+        rows = slice(bases[g], bases[g] + ep_count * blocks[g])
+        cat = jnp.concatenate([ref[cc, rows, :] for cc in range(ctx_count)], axis=1)
+        return jnp.dot(perms[g][...], cat, preferred_element_type=f32).astype(bf16)
+
+    row_set = (sent_rows, got_rows, rows_send, rows_recv)
+    out_set = (sent_out, got_out, out_send, out_recv)
     others = [lax.rem(c + d, ctx_count) for d in range(1, ctx_count)]
 
-    def part_copy(j, d, cc, slot):
+    def part_copy(g, j, d, cc, slot):
+        rows = pl.ds(slot_bases[g], slot_counts[g])
         return pltpu.make_async_remote_copy(
-            src_ref=partial.at[j, cc],
-            dst_ref=got_partial.at[j, slot],
-            send_sem=part_send.at[j, d],
-            recv_sem=part_recv.at[j, slot],
+            src_ref=partial.at[j, cc, rows, :],
+            dst_ref=got_partial.at[j, slot, rows, :],
+            send_sem=part_send.at[g, j, d],
+            recv_sem=part_recv.at[g, j, slot],
             device_id=(cc, e),
             device_id_type=MESH,
         )
 
-    def hid_copy(j, d, cc, slot):
+    def hid_copy(g, j, d, cc, slot):
+        rows = pl.ds(slot_bases[g], slot_counts[g])
         return pltpu.make_async_remote_copy(
-            src_ref=hidden.at[j],
-            dst_ref=got_hidden.at[j, slot],
-            send_sem=hid_send.at[j, d],
-            recv_sem=hid_recv.at[j, slot],
+            src_ref=hidden.at[j, rows, :],
+            dst_ref=got_hidden.at[j, slot, rows, :],
+            send_sem=hid_send.at[g, j, d],
+            recv_sem=hid_recv.at[g, j, slot],
             device_id=(cc, e),
             device_id_type=MESH,
         )
 
+    def begin_rows(g):
+        rows = slice(bases[g], bases[g] + ep_count * blocks[g])
+        placed = jnp.dot(tall[rows, :], normed[...], preferred_element_type=f32).astype(bf16)
+        for cc in range(ctx_count):
+            sent_rows[cc, rows, :] = placed[:, cc * LANES : (cc + 1) * LANES]
+        send_all(g, *row_set)
+
+    def multiply(g, send):
+        receive_all(g, *row_set)
+        ordered = unturned(g, got_rows)
+        count, base = slot_counts[g], slot_bases[g]
+        first = ctx_count * base
+        for cc in range(ctx_count):
+            for k in range(chunks):
+                flat[
+                    first + cc * count : first + (cc + 1) * count, k * LANES : (k + 1) * LANES
+                ] = ordered[k * count : (k + 1) * count, cc * LANES : (cc + 1) * LANES]
+        if g == 0:
+            weight_copies[0].wait()
+            weight_copies[1].wait()
+        rows = flat[first : first + ctx_count * count, :]
+        for j in range(PIECES):
+            cols = slice(j * piece, (j + 1) * piece)
+            gate = jnp.dot(rows, w_gate[:, cols], preferred_element_type=f32).astype(bf16)
+            up = jnp.dot(rows, w_up[:, cols], preferred_element_type=f32).astype(bf16)
+            for cc in range(ctx_count):
+                here = slice(cc * count, (cc + 1) * count)
+                partial[j, cc, base : base + count, 0:piece] = gate[here]
+                partial[j, cc, base : base + count, piece : 2 * piece] = up[here]
+            if send:
+                send_partial(g, j)
+
+    def send_partial(g, j):
+        for d, cc in enumerate(others):
+            part_copy(g, j, d, cc, c).start()
+
+    def activate(g):
+        rows = pl.ds(slot_bases[g], slot_counts[g])
+        for j in range(PIECES):
+            proj = partial[j, c, rows, :].astype(f32)
+            for d, cc in enumerate(others):
+                part_copy(g, j, d, cc, cc).wait_recv()
+                proj += got_partial[j, cc, rows, :].astype(f32)
+            gate, up = proj[:, 0:piece], proj[:, piece : 2 * piece]
+            units_here = (gate / (1.0 + jnp.exp(-gate)) * up).astype(bf16)
+            hidden[j, rows, :] = units_here
+            for d, cc in enumerate(others):
+                hid_copy(g, j, d, cc, c).start()
+            got_hidden[j, c, rows, :] = units_here
+
+    def project_down(g):
+        count, base = slot_counts[g], slot_bases[g]
+        if g == 0:
+            weight_copies[2].wait()
+        down = jnp.zeros((ctx_count * count, wide), f32)
+        for j in range(PIECES):
+            for d, cc in enumerate(others):
+                hid_copy(g, j, d, cc, cc).wait_recv()
+            rows = jnp.concatenate(
+                [got_hidden[j, cc, base : base + count, :] for cc in range(ctx_count)], axis=0
+            )
+            down += jnp.dot(
+                rows, w_down[j * piece : (j + 1) * piece, :], preferred_element_type=f32
+            )
+        down = down.astype(bf16)
+        rows = slice(bases[g], bases[g] + ep_count * blocks[g])
+        for cc in range(ctx_count):
+            for k in range(chunks):
+                turned[
+                    bases[g] + k * count : bases[g] + (k + 1) * count,
+                    cc * LANES : (cc + 1) * LANES,
+                ] = down[cc * count : (cc + 1) * count, k * LANES : (k + 1) * LANES]
+        back = jnp.dot(perms_t[g][...], turned[rows, :], preferred_element_type=f32).astype(bf16)
+        for cc in range(ctx_count):
+            sent_out[cc, rows, :] = back[:, cc * LANES : (cc + 1) * LANES]
+        send_all(g, *out_set)
+
+    def take_back(g):
+        receive_all(g, *out_set)
+        ordered = unturned(g, got_out)
+        count, base = slot_counts[g], slot_bases[g]
+        for cc in range(ctx_count):
+            for k in range(chunks):
+                cols = slice(cc * wide + k * LANES, cc * wide + (k + 1) * LANES)
+                expert_out[base : base + count, cols] = ordered[
+                    k * count : (k + 1) * count, cc * LANES : (cc + 1) * LANES
+                ]
+
+    begin_rows(0)
+    begin_rows(1)
+    multiply(0, True)
+    multiply(1, False)
+    activate(0)
     for j in range(PIECES):
-        cols = slice(j * piece, (j + 1) * piece)
-        gate = jnp.dot(flat[...], w_gate[:, cols], preferred_element_type=f32).astype(bf16)
-        up = jnp.dot(flat[...], w_up[:, cols], preferred_element_type=f32).astype(bf16)
-        for cc in range(ctx_count):
-            partial[j, cc, :, 0:piece] = gate[cc * slots : (cc + 1) * slots]
-            partial[j, cc, :, piece : 2 * piece] = up[cc * slots : (cc + 1) * slots]
-        for d, cc in enumerate(others):
-            part_copy(j, d, cc, c).start()
-
-    for j in range(PIECES):
-        proj = partial[j, c].astype(f32)
-        for d, cc in enumerate(others):
-            part_copy(j, d, cc, cc).wait_recv()
-            proj += got_partial[j, cc].astype(f32)
-        gate, up = proj[:, 0:piece], proj[:, piece : 2 * piece]
-        hidden[j] = (gate / (1.0 + jnp.exp(-gate)) * up).astype(bf16)
-        for d, cc in enumerate(others):
-            hid_copy(j, d, cc, c).start()
-        got_hidden[j, c] = hidden[j]
-
-    weight_copies[2].wait()
-    down = jnp.zeros((ctx_count * slots, wide), f32)
-    for j in range(PIECES):
-        for d, cc in enumerate(others):
-            hid_copy(j, d, cc, cc).wait_recv()
-        rows = jnp.concatenate([got_hidden[j, cc] for cc in range(ctx_count)], axis=0)
-        down += jnp.dot(
-            rows, w_down[j * piece : (j + 1) * piece, :], preferred_element_type=f32
-        )
-    down = down.astype(bf16)
-    for cc in range(ctx_count):
-        for k in range(chunks):
-            turned[k * slots : (k + 1) * slots, cc * LANES : (cc + 1) * LANES] = down[
-                cc * slots : (cc + 1) * slots, k * LANES : (k + 1) * LANES
-            ]
-    back = jnp.dot(perm_t_ref[...], turned[...], preferred_element_type=f32).astype(bf16)
-    for cc in range(ctx_count):
-        sent_out[cc] = back[:, cc * LANES : (cc + 1) * LANES]
-    all_exchange(sent_out, got_out, out_send, out_recv)
-    ordered = unturned(got_out)
-    for cc in range(ctx_count):
-        for k in range(chunks):
-            cols = slice(cc * wide + k * LANES, cc * wide + (k + 1) * LANES)
-            expert_out[:, cols] = ordered[k * slots : (k + 1) * slots, cc * LANES : (cc + 1) * LANES]
-
-    hits = jnp.zeros((tokens, slots), f32)
-    mix = jnp.zeros((tokens, slots), f32)
-    for j in range(ids_ref.shape[1]):
-        hit = ids_ref[:, j : j + 1] == col_meta_ref[0:1, :]
-        hits += jnp.where(hit, 1.0, 0.0)
-        mix += jnp.where(hit, gates_ref[:, j : j + 1], 0.0)
-    count = jnp.dot(lower_ref[...], hits.astype(bf16), preferred_element_type=f32)
-    mix = jnp.where(count.astype(jnp.int32) == col_meta_ref[1:2, :] + 1, mix, 0.0)
-    high = mix.astype(bf16)
-    low = (mix - high.astype(f32)).astype(bf16)
-    both = jnp.concatenate([high, low], axis=0)
+        send_partial(1, j)
+    project_down(0)
+    activate(1)
+    project_down(1)
+    take_back(0)
+    take_back(1)
+
     for cc in range(ctx_count):
         cols = slice(cc * wide, (cc + 1) * wide)
-        mixed = jnp.dot(both, expert_out[:, cols], preferred_element_type=f32)
+        mixed = lax.dot_general(
+            mix[...], expert_out[:, cols], (((0,), (0,)), ((), ())), preferred_element_type=f32
+        )
         out_ref[:, cols] = (context[:, cols] + mixed[0:tokens] + mixed[tokens:]).astype(bf16)
 
-    for copy_set in (
-        (sent_rows, got_rows, rows_send, rows_recv),
-        (sent_out, got_out, out_send, out_recv),
-    ):
-        all_sent(*copy_set)
-    for j in range(PIECES):
-        for d, cc in enumerate(others):
-            part_copy(j, d, cc, c).wait_send()
-            hid_copy(j, d, cc, c).wait_send()
+    for g in groups:
+        all_sent(g, *row_set)
+        all_sent(g, *out_set)
+        for j in range(PIECES):
+            for d, cc in enumerate(others):
+                part_copy(g, j, d, cc, c).wait_send()
+                hid_copy(g, j, d, cc, c).wait_send()
 
 
 def local_fused(
@@ -508,26 +564,32 @@
     chunks = wide // LANES
     slots = ep_count * CAP
     tall_rows = chunks * slots
-    n = np.arange(tall_rows)
-    row_e, row_k, row_s = n // (chunks * CAP), n // CAP % chunks, n % CAP
-    row_meta = np.stack([row_e, row_k, row_s], axis=1).astype(np.int32)
-    m = np.arange(slots)
-    col_meta = np.stack([m // CAP, m % CAP], axis=0).astype(np.int32)
-    lower = np.tril(np.ones((tokens, tokens), np.float32))
-    perm = np.zeros((tall_rows, tall_rows), np.float32)
-    perm[row_k * slots + row_e * CAP + row_s, n] = 1.0
+    row_meta, slot_meta, perms = [], [], []
+    for g, size in enumerate(SLOT_GROUPS):
+        first = sum(SLOT_GROUPS[:g])
+        n = np.arange(ep_count * chunks * size)
+        row_e, row_k, row_s = n // (chunks * size), n // size % chunks, n % size
+        row_meta.append(np.stack([row_e, row_k, row_s + first], axis=1).astype(np.int32))
+        m = np.arange(ep_count * size)
+        slot_meta.append(np.stack([m // size, m % size + first], axis=1).astype(np.int32))
+        perm = np.zeros((n.size, n.size), np.float32)
+        perm[(row_k * ep_count + row_e) * size + row_s, n] = 1.0
+        perms.append(perm)
+    row_meta, slot_meta = np.concatenate(row_meta), np.concatenate(slot_meta)
+    upper = np.triu(np.ones((tokens, tokens), np.float32))
     vmem = pl.BlockSpec(memory_space=pltpu.VMEM)
     anywhere = pl.BlockSpec(memory_space=pl.ANY)
     dma = pltpu.SemaphoreType.DMA
     devices = ctx_count * ep_count
+    groups = len(SLOT_GROUPS)
     piece = units // PIECES
     across = ctx_count * LANES
     out = pl.pallas_call(
         functools.partial(fused, ctx_count, ep_count),
         out_shape=jax.ShapeDtypeStruct((tokens, D), bf16),
-        in_specs=[vmem] * 3
+        in_specs=[vmem] * 2
         + [pl.BlockSpec(memory_space=pltpu.SMEM)]
-        + [vmem] * 10
+        + [vmem] * 11
         + [anywhere] * 3,
         out_specs=vmem,
         scratch_shapes=[
@@ -546,20 +608,21 @@
             pltpu.VMEM((ctx_count, tall_rows, LANES), bf16),
             pltpu.VMEM((ctx_count, tall_rows, LANES), bf16),
             pltpu.VMEM((slots, D), bf16),
+            pltpu.VMEM((slots, 2 * tokens), bf16),
             pltpu.VMEM((wide, units), bf16),
             pltpu.VMEM((wide, units), bf16),
             pltpu.VMEM((units, wide), bf16),
             dma((3,)),
             dma((2,)),
             dma((2,)),
-            dma((devices,)),
-            dma((devices,)),
-            dma((PIECES, ctx_count)),
-            dma((PIECES, ctx_count)),
-            dma((PIECES, ctx_count)),
-            dma((PIECES, ctx_count)),
-            dma((devices,)),
-            dma((devices,)),
+            dma((groups, devices)),
+            dma((groups, devices)),
+            dma((groups, PIECES, ctx_count)),
+            dma((groups, PIECES, ctx_count)),
+            dma((groups, PIECES, ctx_count)),
+            dma((groups, PIECES, ctx_count)),
+            dma((groups, devices)),
+            dma((groups, devices)),
         ],
         compiler_params=pltpu.CompilerParams(
             collective_id=0, has_side_effects=True, vmem_limit_bytes=56 * 1024 * 1024
@@ -568,20 +631,20 @@
             flops=4_000_000_000, bytes_accessed=14_000_000, transcendentals=1_000_000
         ),
     )(
-        expert_ids[0],
         expert_ids[0].T,
-        gate_weights[0],
+        gate_weights[0].T,
         trace_lengths,
         queries[0],
         key_heads[0],
         value_head_array[0],
         norm_gain[None],
         row_meta,
-        col_meta,
-        lower.astype(bf16),
-        lower.T.astype(bf16),
-        perm.astype(bf16),
-        perm.T.astype(bf16),
+        slot_meta,
+        upper.astype(bf16),
+        perms[0].astype(bf16),
+        perms[1].astype(bf16),
+        perms[0].T.astype(bf16),
+        perms[1].T.astype(bf16),
         w_gate,
         w_up,
         w_down,
@@ -592,7 +655,7 @@
 def local(*args):
     ctx_count, ep_count = lax.axis_size("ctx"), lax.axis_size("ep")
     wide, units = args[7].shape
-    aligned = (wide // LANES * CAP) % 16 == 0 and units % (PIECES * LANES) == 0
+    aligned = all((wide // LANES * size) % 16 == 0 for size in SLOT_GROUPS) and units % (PIECES * LANES) == 0
     if ep_count == EXP_WIN and ctx_count == 4 and aligned:
         return local_fused(*args)
     return local_plain(*args)

time: 100 us -> 91.9 us (0.919)
  Pallas kernels: 93.5 us -> 88.1 us
  local copies, waits for them, and re-layouts: 6.42 us -> 3.6 us
    pallas_call x1, Pallas kernels: 93.5 us -> 88.1 us  [local_fused(): pl.pallas_call(functools.partial(fused, ctx_count, ep_count), out_shape=j...]
    squeeze x1 -> x0, local copies, waits for them, and re-layouts: 1.41 us -> none  [local_fused(): expert_ids[0]]
    unnamed x2 -> x1, local copies, waits for them, and re-layouts: 3.69 us -> 2.29 us
where the time goes in v3:
time: 91.9 us; the launch traced here: 91.7 us
  Pallas kernels  88.1 us (96%)
  local copies, waits for them, and re-layouts  3.6 us (4%)
    pallas_call x1, Pallas kernels, local_fused(): pl.pallas_call(functools.partial(fused, ctx_count, ep_count), out_shape=j...  88.1 us
    unnamed x1, local copies, waits for them, and re-layouts  2.29 us

profile of v3, /device:TPU:0, one launch (start us, length us, event | category | flops | bytes accessed | tf_op | source)
XLA Modules:
  0.0 91.7 jit_solution(17997355298432859891)
XLA Ops:
  0.0 1.3 %broadcast_in_dim.6.gain_ref = bf16[1,4096]{1,0:T(2,128)(2,1)} reshape(bf16[4096]{0:T(1024)(128)(2,1)} %param.23) | data formatting | bytes 16384 | tf_op jit(solution)/shard_map/broadcast_in_dim | solution.py:640
  1.3 88.1 %shard_map.163 = bf16[128,4096]{1,0:T(8,128)(2,1)} custom-call(s32[8,128]{1,0:T(8,128)} %bitcast.14, f32[8,128]{1,0:T(8,128)} %bitcast.15, s32[1,6]{1,0:T(1,128)} %lengths_ref.1, bf16[128,4096]{1,0:T(8,128)(2,1)} %bitcast.11, bf16[128,256]{1,0:T(8,128)(2,1)} %bitcast.12, bf16[128,256]{1,0:T(8,128)(2,1)} %bitcast.13, ...), custom_call_target="tpu_custom_call" | custom-call | flops 4000000000 | bytes 14000000 | tf_op jit(solution)/shard_map/pallas_call | solution.py:587
  89.4 2.3 %copy.19 = bf16[1,128,4096]{2,1,0:T(8,128)(2,1)} copy(bf16[1,128,4096]{2,1,0:T(8,128)(2,1)} %bitcast.10) | data formatting | bytes 2097152

commit v4 on v3

--- a/solution.py
+++ b/solution.py
@@ -193,6 +193,8 @@
     w_down_hbm,
     out_ref,
     kv_prev,
+    tops,
+    totals,
     context,
     normed,
     tall,
@@ -261,15 +263,46 @@
         return carry
 
     lax.fori_loop(1, devices, greet, 0)
-    named = jnp.zeros((chunks * slots, tokens), f32)
-    for j in range(ids_ref.shape[0]):
-        named += jnp.where(ids_ref[j : j + 1, :] == row_meta_ref[:, 0:1], 1.0, 0.0)
-    count = jnp.dot(named.astype(bf16), upper_ref[...], preferred_element_type=f32)
-    taken = jnp.where(count.astype(jnp.int32) == row_meta_ref[:, 2:3] + 1, named, 0.0)
-    for k in range(chunks):
-        tall[:, k * tokens : (k + 1) * tokens] = jnp.where(
-            row_meta_ref[:, 1:2] == k, taken, 0.0
-        ).astype(bf16)
+    square = (tokens, tokens)
+    query_pos = c * tokens + lax.broadcasted_iota(jnp.int32, square, 0)
+    key_pos = c * tokens + lax.broadcasted_iota(jnp.int32, square, 1)
+    first_pos = jnp.zeros(square, jnp.int32)
+    start = jnp.int32(0)
+    for i in range(lengths_ref.shape[1]):
+        first_pos = jnp.where(query_pos >= start, start, first_pos)
+        start = start + lengths_ref[0, i]
+    own_visible = (key_pos <= query_pos) & (key_pos >= first_pos)
+    earlier_visible = key_pos - tokens >= first_pos
+    score_scale = 1.0 / math.sqrt(HEAD_SIZE)
+
+    def score(cols, keys, visible):
+        scores = lax.dot_general(
+            q_ref[:, cols], keys, (((1,), (1,)), ((), ())), preferred_element_type=f32
+        )
+        return jnp.where(visible, scores * score_scale, -1e30)
+
+    def head_cols(head):
+        return pl.ds(pl.multiple_of(head * HEAD_SIZE, HEAD_SIZE), HEAD_SIZE)
+
+    for kv in range(KEY_VALUE_HEADS):
+        kv_cols = slice(kv * HEAD_SIZE, (kv + 1) * HEAD_SIZE)
+
+        def attend_own(h, carry, kv=kv, keys=k_ref[:, kv_cols], values=v_ref[:, kv_cols]):
+            for one in range(4):
+                head = kv * head_groups + h * 4 + one
+                cols = head_cols(head)
+                scores = score(cols, keys, own_visible)
+                top = jnp.max(scores, axis=-1, keepdims=True)
+                weights = jnp.where(own_visible, jnp.exp(scores - top), 0.0)
+                total = jnp.sum(weights, axis=-1, keepdims=True)
+                tops[head] = jnp.broadcast_to(top, (tokens, HEAD_SIZE))
+                totals[head] = jnp.broadcast_to(total, (tokens, HEAD_SIZE))
+                context[:, cols] = jnp.dot(
+                    weights.astype(bf16), values, preferred_element_type=f32
+                )
+            return carry
+
+        lax.fori_loop(0, head_groups // 4, attend_own, 0)
 
     pl.semaphore_wait(barrier, devices - 1)
 
@@ -299,40 +332,39 @@
     mix[:, 0:tokens] = high
     mix[:, tokens : 2 * tokens] = (gate_at - high.astype(f32)).astype(bf16)
 
-    query_pos = c * tokens + lax.broadcasted_iota(jnp.int32, (tokens, 2 * tokens), 0)
-    key_pos = (c - 1) * tokens + lax.broadcasted_iota(jnp.int32, (tokens, 2 * tokens), 1)
-    first_pos = jnp.zeros((tokens, 2 * tokens), jnp.int32)
-    start = jnp.int32(0)
-    for i in range(lengths_ref.shape[1]):
-        first_pos = jnp.where(query_pos >= start, start, first_pos)
-        start = start + lengths_ref[0, i]
-    visible = (key_pos <= query_pos) & (key_pos >= first_pos)
-    score_scale = 1.0 / math.sqrt(HEAD_SIZE)
+    named = jnp.zeros((chunks * slots, tokens), f32)
+    for j in range(ids_ref.shape[0]):
+        named += jnp.where(ids_ref[j : j + 1, :] == row_meta_ref[:, 0:1], 1.0, 0.0)
+    count = jnp.dot(named.astype(bf16), upper_ref[...], preferred_element_type=f32)
+    taken = jnp.where(count.astype(jnp.int32) == row_meta_ref[:, 2:3] + 1, named, 0.0)
+    for k in range(chunks):
+        tall[:, k * tokens : (k + 1) * tokens] = jnp.where(
+            row_meta_ref[:, 1:2] == k, taken, 0.0
+        ).astype(bf16)
 
     for copy in kv_copies:
         copy.wait()
 
     for kv in range(KEY_VALUE_HEADS):
         kv_cols = slice(kv * HEAD_SIZE, (kv + 1) * HEAD_SIZE)
-        keys = jnp.concatenate([kv_prev[0, :, kv_cols], k_ref[:, kv_cols]], axis=0)
-        values = jnp.concatenate([kv_prev[1, :, kv_cols], v_ref[:, kv_cols]], axis=0)
-
-        def attend(h, carry, kv=kv, keys=keys, values=values):
+
+        def attend_earlier(
+            h, carry, kv=kv, keys=kv_prev[0, :, kv_cols], values=kv_prev[1, :, kv_cols]
+        ):
             for one in range(4):
                 head = kv * head_groups + h * 4 + one
-                cols = pl.ds(pl.multiple_of(head * HEAD_SIZE, HEAD_SIZE), HEAD_SIZE)
-                scores = lax.dot_general(
-                    q_ref[:, cols], keys, (((1,), (1,)), ((), ())), preferred_element_type=f32
-                )
-                scores = jnp.where(visible, scores * score_scale, -1e30)
-                top = jnp.max(scores, axis=-1, keepdims=True)
-                weights = jnp.where(visible, jnp.exp(scores - top), 0.0)
-                total = jnp.sum(weights, axis=-1, keepdims=True)
+                cols = head_cols(head)
+                scores = score(cols, keys, earlier_visible)
+                old_top = tops[head]
+                top = jnp.maximum(old_top, jnp.max(scores, axis=-1, keepdims=True))
+                weights = jnp.where(earlier_visible, jnp.exp(scores - top), 0.0)
+                rescale = jnp.exp(old_top - top)
+                total = totals[head] * rescale + jnp.sum(weights, axis=-1, keepdims=True)
                 summed = jnp.dot(weights.astype(bf16), values, preferred_element_type=f32)
-                context[:, cols] = summed / total
+                context[:, cols] = (context[:, cols] * rescale + summed) / total
             return carry
 
-        lax.fori_loop(0, head_groups // 4, attend, 0)
+        lax.fori_loop(0, head_groups // 4, attend_earlier, 0)
 
     def add_square(h, running):
         part = context[:, pl.ds(pl.multiple_of(h * HEAD_SIZE, HEAD_SIZE), HEAD_SIZE)]
@@ -428,15 +460,16 @@
             device_id_type=MESH,
         )
 
-    def begin_rows(g):
+    def place_rows(g):
         rows = slice(bases[g], bases[g] + ep_count * blocks[g])
         placed = jnp.dot(tall[rows, :], normed[...], preferred_element_type=f32).astype(bf16)
         for cc in range(ctx_count):
             sent_rows[cc, rows, :] = placed[:, cc * LANES : (cc + 1) * LANES]
-        send_all(g, *row_set)
 
     def multiply(g, send):
         receive_all(g, *row_set)
+        if g == 0:
+            send_all(1, *row_set)
         ordered = unturned(g, got_rows)
         count, base = slot_counts[g], slot_bases[g]
         first = ctx_count * base
@@ -492,6 +525,9 @@
             down += jnp.dot(
                 rows, w_down[j * piece : (j + 1) * piece, :], preferred_element_type=f32
             )
+        if g == 0:
+            for j in range(PIECES):
+                send_partial(1, j)
         down = down.astype(bf16)
         rows = slice(bases[g], bases[g] + ep_count * blocks[g])
         for cc in range(ctx_count):
@@ -516,13 +552,12 @@
                     k * count : (k + 1) * count, cc * LANES : (cc + 1) * LANES
                 ]
 
-    begin_rows(0)
-    begin_rows(1)
+    place_rows(0)
+    send_all(0, *row_set)
+    place_rows(1)
     multiply(0, True)
     multiply(1, False)
     activate(0)
-    for j in range(PIECES):
-        send_partial(1, j)
     project_down(0)
     activate(1)
     project_down(1)
@@ -594,6 +629,8 @@
         out_specs=vmem,
         scratch_shapes=[
             pltpu.VMEM((2, tokens, KEY_VALUE_HEADS * HEAD_SIZE), bf16),
+            pltpu.VMEM((QUERY_HEADS, tokens, HEAD_SIZE), jnp.float32),
+            pltpu.VMEM((QUERY_HEADS, tokens, HEAD_SIZE), jnp.float32),
             pltpu.VMEM((tokens, D), jnp.float32),
             pltpu.VMEM((chunks * tokens, across), bf16),
             pltpu.VMEM((tall_rows, chunks * tokens), bf16),
@@ -656,6 +693,7 @@
     ctx_count, ep_count = lax.axis_size("ctx"), lax.axis_size("ep")
     wide, units = args[7].shape
     aligned = all((wide // LANES * size) % 16 == 0 for size in SLOT_GROUPS) and units % (PIECES * LANES) == 0
+    aligned = aligned and args[0].shape[1] == HEAD_SIZE
     if ep_count == EXP_WIN and ctx_count == 4 and aligned:
         return local_fused(*args)
     return local_plain(*args)

time: 91.9 us -> 102 us (1.11)
  Pallas kernels: 88.1 us -> 97.7 us
    pallas_call x1, Pallas kernels: 88.1 us -> 97.7 us  [local_fused(): pl.pallas_call(functools.partial(fused, ctx_count, ep_count), out_shape=j...]
where the time goes in v4:
time: 102 us; the launch traced here: 101 us
  Pallas kernels  97.7 us (96%)
  local copies, waits for them, and re-layouts  3.6 us (4%)
    pallas_call x1, Pallas kernels, local_fused(): pl.pallas_call(functools.partial(fused, ctx_count, ep_count), out_shape=j...  97.7 us
    unnamed x1, local copies, waits for them, and re-layouts  2.29 us

profile of v4, /device:TPU:0, one launch (start us, length us, event | category | flops | bytes accessed | tf_op | source)
XLA Modules:
  0.0 101.3 jit_solution(12800792969286218462)
XLA Ops:
  0.0 1.3 %broadcast_in_dim.6.gain_ref = bf16[1,4096]{1,0:T(2,128)(2,1)} reshape(bf16[4096]{0:T(1024)(128)(2,1)} %param.23) | data formatting | bytes 16384 | tf_op jit(solution)/shard_map/broadcast_in_dim | solution.py:677
  1.3 97.7 %shard_map.163 = bf16[128,4096]{1,0:T(8,128)(2,1)} custom-call(s32[8,128]{1,0:T(8,128)} %bitcast.14, f32[8,128]{1,0:T(8,128)} %bitcast.15, s32[1,6]{1,0:T(1,128)} %lengths_ref.1, bf16[128,4096]{1,0:T(8,128)(2,1)} %bitcast.11, bf16[128,256]{1,0:T(8,128)(2,1)} %bitcast.12, bf16[128,256]{1,0:T(8,128)(2,1)} %bitcast.13, ...), custom_call_target="tpu_custom_call" | custom-call | flops 4000000000 | bytes 14000000 | tf_op jit(solution)/shard_map/pallas_call | solution.py:622
  99.1 2.3 %copy.19 = bf16[1,128,4096]{2,1,0:T(8,128)(2,1)} copy(bf16[1,128,4096]{2,1,0:T(8,128)(2,1)} %bitcast.10) | data formatting | bytes 2097152
